TPU v7x, 128 devices: a whole 4x4x4 slice. The times are simulated.
128 devices in a mesh: ctx: 16 (over z_lo, y, core), tp: 4 (over x), fsdp: 2 (over z_hi).
Axes of the slice: x: 4, y: 4, z: 4 (z_hi: 2, z_lo: 2; z = z_hi * 2 + z_lo), core: 2. Of those that a mesh axis runs over, the one named last changes fastest.
Arguments:
- x_input: bfloat16 [2, 4096, 128, 128], P('fsdp', 'ctx', 'tp'), may hold values from -6 to 6
- gate_input: bfloat16 [2, 4096, 128, 128], P('fsdp', 'ctx', 'tp'), may hold values from -6 to 6
- dt_raw: bfloat16 [2, 128, 4096], P('fsdp', 'tp', 'ctx'), may hold values from -4 to 4
- b_input: bfloat16 [2, 4096, 8, 128], P('fsdp', 'ctx', 'tp'), may hold values from -6 to 6
- c_input: bfloat16 [2, 4096, 8, 128], P('fsdp', 'ctx', 'tp'), may hold values from -0.5 to 0.5
- a_log: float32 [128], P('tp'), may hold values from -9 to -3
- dt_bias: float32 [128], P('tp'), may hold values from -1 to 1
- skip_weight: float32 [128], P('tp'), may hold values from 0.5 to 1.5
- norm_gain: float32 [16384], P(('tp', 'fsdp')), may hold values from 0.1 to 1.9
- valid_len: int32 [2], P('fsdp'), may hold values from 2048 to 4096, as said below
- grad_output: bfloat16 [2, 4096, 128, 128], P('fsdp', 'ctx', 'tp'), may hold values from -6 to 6
Outputs:
- grad_x: bfloat16 [2, 4096, 128, 128], P('fsdp', 'ctx', 'tp')
- grad_gate: bfloat16 [2, 4096, 128, 128], P('fsdp', 'ctx', 'tp')
- grad_dt: bfloat16 [2, 128, 4096], P('fsdp', 'tp', 'ctx')
- grad_b: bfloat16 [2, 4096, 8, 128], P('fsdp', 'ctx', 'tp')
- grad_c: bfloat16 [2, 4096, 8, 128], P('fsdp', 'ctx', 'tp')
- grad_a_log: float32 [128], P('tp')
- grad_dt_bias: float32 [128], P('tp')
- grad_skip: float32 [128], P('tp')
- grad_gain: float32 [16384], P(('tp', 'fsdp'))
Inputs may be any that keep to these rules, and one draw needn't show every extreme that they name: `valid_len`: the sequences' valid lengths are all different, and the longest is 4096.
All inputs are finite; a program needn't handle non-finite values.
Results may differ from a plain program's by a relative error of at most 0.002.
Values sent between devices are 32-bit elements; how exact they have to be, the bound alone decides.
A program may use at most 192 MiB of HBM per device.

v0:
```python
import math

import jax
import jax.numpy as jnp
from jax import lax
from jax.sharding import PartitionSpec as P

EPS = 1e-05
HIGH = lax.Precision.HIGHEST


def prefix(part, axis, combine, identity, reverse):
    count = lax.axis_size(axis)
    place = lax.axis_index(axis)
    ahead = count - 1 - place if reverse else place
    gathered = jax.tree.map(lambda a: lax.all_gather(a, axis), part)
    state = jax.tree.map(lambda a, e: jnp.zeros_like(a) + jnp.asarray(e, a.dtype), part, identity)

    def one(hop, state):
        source = count - 1 - hop if reverse else hop
        return combine(
            state, jax.tree.map(lambda a: lax.dynamic_index_in_dim(a, source, 0, False), gathered)
        )

    return lax.fori_loop(0, ahead, one, state)


def block_step(decay_rate, carry_state, x_block, step_block, b_block, c_block):
    block_len = step_block.shape[-1]
    running = jnp.cumsum(step_block * decay_rate[..., None], axis=-1)
    log_gaps = running[..., :, None] - running[..., None, :]
    causal = jnp.arange(block_len)[:, None] >= jnp.arange(block_len)[None, :]
    decay_mask = jnp.where(causal, jnp.exp(jnp.where(causal, log_gaps, 0.0)), 0.0)
    scores = jnp.einsum("tgn,sgn->gts", c_block, b_block, precision=HIGH)
    weights = decay_mask * scores[:, None] * step_block[:, :, None, :]
    output = jnp.einsum("gkts,sgkp->tgkp", weights, x_block, precision=HIGH)
    carried = jnp.einsum("tgn,gkpn->tgkp", c_block, carry_state, precision=HIGH)
    output = output + carried * jnp.transpose(jnp.exp(running), (2, 0, 1))[..., None]
    weighting = jnp.exp(running[..., -1:] - running) * step_block
    fresh_state = jnp.einsum("gks,sgkp,sgn->gkpn", weighting, x_block, b_block, precision=HIGH)
    next_state = jnp.exp(running[..., -1])[..., None, None] * carry_state + fresh_state
    return (next_state, output)


def run_blocks(decay_rate, start_state, x_all, step_all, b_all, c_all, block_len):
    length = x_all.shape[0]
    blocks = length // block_len
    x_blocks = x_all.reshape((blocks, block_len) + x_all.shape[1:])
    step_blocks = jnp.moveaxis(step_all.reshape(step_all.shape[:2] + (blocks, block_len)), 2, 0)
    b_blocks = b_all.reshape((blocks, block_len) + b_all.shape[1:])
    c_blocks = c_all.reshape((blocks, block_len) + c_all.shape[1:])

    def advance(carry_state, pieces):
        return block_step(decay_rate, carry_state, pieces[0], pieces[1], pieces[2], pieces[3])

    final_state, outputs = lax.scan(
        advance, start_state, (x_blocks, step_blocks, b_blocks, c_blocks)
    )
    return outputs.reshape((length,) + outputs.shape[2:])


def mixer_forward(
    x_all,
    step_raw,
    b_all,
    c_all,
    gate_all,
    a_log,
    dt_bias,
    skip_weight,
    norm_gain,
    start_state,
    block_len,
):
    step_size = jax.nn.softplus(step_raw + dt_bias[..., None])
    decay_rate = -jnp.exp(a_log)
    scanned = run_blocks(decay_rate, start_state, x_all, step_size, b_all, c_all, block_len)
    mixed = scanned + skip_weight[None, :, :, None] * x_all
    gated = mixed * jax.nn.silu(gate_all)
    mean_square = jnp.mean(gated * gated, axis=(2, 3), keepdims=True)
    return gated * lax.rsqrt(mean_square + EPS) * norm_gain[None]


def local_states(x_all, step_raw, b_all, a_log, dt_bias):
    step_size = jax.nn.softplus(step_raw + dt_bias[..., None])
    log_steps = step_size * (-jnp.exp(a_log))[..., None]
    running = jnp.cumsum(log_steps, axis=-1)
    log_total = running[..., -1]
    weighting = jnp.exp(log_total[..., None] - running) * step_size
    fresh_state = jnp.einsum("gks,sgkp,sgn->gkpn", weighting, x_all, b_all, precision=HIGH)
    return (log_total, fresh_state)


def join_states(earlier, later):
    return (earlier[0] + later[0], later[1] + jnp.exp(later[0])[..., None, None] * earlier[1])


def prefix_states(log_total, states, backward):
    heads_here = states.shape[0] * states.shape[1]
    flat_log = log_total.reshape(heads_here)
    flat_states = states.reshape((heads_here,) + states.shape[2:])
    identity = (jnp.zeros_like(flat_log), jnp.zeros_like(flat_states))
    _, result = prefix((flat_log, flat_states), "ctx", join_states, identity, backward)
    return result.reshape(states.shape)


def per_device(
    x_input,
    gate_input,
    dt_raw,
    b_input,
    c_input,
    a_log,
    dt_bias,
    skip_weight,
    norm_gain,
    valid_len,
    grad_output,
):
    tokens = x_input.shape[1]
    heads_here = x_input.shape[2]
    head_dim = x_input.shape[3]
    groups_here = b_input.shape[2]
    per_group = heads_here // groups_here
    block_len = math.gcd(256, tokens)
    gain_rows = lax.all_gather(norm_gain, "fsdp", axis=0, tiled=True)
    x_all = x_input[0].astype(jnp.float32).reshape(tokens, groups_here, per_group, head_dim)
    gate_all = gate_input[0].astype(jnp.float32).reshape(tokens, groups_here, per_group, head_dim)
    step_raw = dt_raw[0].astype(jnp.float32).reshape(groups_here, per_group, tokens)
    b_all = b_input[0].astype(jnp.float32)
    c_all = c_input[0].astype(jnp.float32)
    a_grp = a_log.reshape(groups_here, per_group)
    bias_grp = dt_bias.reshape(groups_here, per_group)
    skip_grp = skip_weight.reshape(groups_here, per_group)
    gain_grp = gain_rows.reshape(groups_here, per_group, head_dim)
    offset = lax.axis_index("ctx") * tokens
    keep_mask = (offset + jnp.arange(tokens, dtype=jnp.int32) < valid_len[0]).astype(jnp.float32)
    cotangent = grad_output[0].astype(jnp.float32).reshape(tokens, groups_here, per_group, head_dim)
    cotangent = cotangent * keep_mask[:, None, None, None]
    totals, state_pull = jax.vjp(local_states, x_all, step_raw, b_all, a_grp, bias_grp)
    log_total, fresh_state = totals
    carried = prefix_states(log_total, fresh_state, False)

    def local_out(
        x_value,
        step_value,
        b_value,
        c_value,
        gate_value,
        a_value,
        bias_value,
        skip_value,
        gain_value,
        start_state,
    ):
        return mixer_forward(
            x_value,
            step_value,
            b_value,
            c_value,
            gate_value,
            a_value,
            bias_value,
            skip_value,
            gain_value,
            start_state,
            block_len,
        )

    _, out_pull = jax.vjp(
        local_out,
        x_all,
        step_raw,
        b_all,
        c_all,
        gate_all,
        a_grp,
        bias_grp,
        skip_grp,
        gain_grp,
        carried,
    )
    grads_out = out_pull(cotangent)
    behind = prefix_states(log_total, grads_out[9], True)
    grad_log = jnp.sum(behind * carried, axis=(2, 3)) * jnp.exp(log_total)
    grads_state = state_pull((grad_log, behind))
    grad_x = grads_out[0] + grads_state[0]
    grad_step = grads_out[1] + grads_state[1]
    grad_b = grads_out[2] + grads_state[2]
    grad_a = (grads_out[5] + grads_state[3]).reshape(heads_here)
    grad_bias = (grads_out[6] + grads_state[4]).reshape(heads_here)
    grad_skip = grads_out[7].reshape(heads_here)
    grad_gain = grads_out[8].reshape(heads_here * head_dim)
    head_totals = lax.psum((grad_a, grad_bias, grad_skip), ("ctx", "fsdp"))
    gain_part = lax.psum_scatter(grad_gain, "fsdp", scatter_dimension=0, tiled=True)
    gain_total = lax.psum(gain_part, "ctx")
    scale = 1.0 / math.sqrt(tokens * lax.axis_size("ctx") * lax.axis_size("fsdp"))
    return (
        grad_x.reshape(1, tokens, heads_here, head_dim).astype(jnp.bfloat16),
        grads_out[4].reshape(1, tokens, heads_here, head_dim).astype(jnp.bfloat16),
        grad_step.reshape(1, heads_here, tokens).astype(jnp.bfloat16),
        grad_b[None].astype(jnp.bfloat16),
        grads_out[3][None].astype(jnp.bfloat16),
        head_totals[0] * scale,
        head_totals[1] * scale,
        head_totals[2] * scale,
        gain_total * scale,
    )


def solution(mesh):
    placed = (
        P("fsdp", "ctx", "tp", None),
        P("fsdp", "ctx", "tp", None),
        P("fsdp", "tp", "ctx"),
        P("fsdp", "ctx", "tp", None),
        P("fsdp", "ctx", "tp", None),
        P("tp"),
        P("tp"),
        P("tp"),
        P(("tp", "fsdp")),
        P("fsdp"),
        P("fsdp", "ctx", "tp", None),
    )
    return jax.shard_map(
        per_device,
        mesh=mesh,
        in_specs=placed,
        out_specs=(
            P("fsdp", "ctx", "tp", None),
            P("fsdp", "ctx", "tp", None),
            P("fsdp", "tp", "ctx"),
            P("fsdp", "ctx", "tp", None),
            P("fsdp", "ctx", "tp", None),
            P("tp"),
            P("tp"),
            P("tp"),
            P(("tp", "fsdp")),
        ),
        check_vma=False,
    )
```

profile of v0, /device:TPU:1, one launch (start us, length us, event | category | flops | bytes accessed | tf_op | source)
XLA Modules:
  0.0 644.3 jit_solution(6440168016679897009)
XLA Ops:
  10.3 1.1 reduce-window.50
  12.8 3.0 copy.233
  15.8 3.5 fusion.8
  20.4 1.1 reduce-window.48
  23.5 4.9 copy.243
  29.7 5.2 copy.226
  34.9 21.7 %all-gather = f32[16,1,32]{2,1,0:T(1,128)} all-gather(f32[1,1,32]{2,1,0:T(1,128)S(1)} %reshape.554), channel_id=1, replica_groups=mesh['ctx'=16,'tp'=4,'fsdp'=2] {'ctx'}, dimensions={0}, use_global_device_ids=true | all-gather | bytes 2176 | tf_op jit(solution)/shard_map/all_gather | solution.py:16
  56.6 5.1 all_gather.13
  62.9 1.0 fusion.95
  63.9 130.1 %all-gather.4.cloned.1.call-done = f32[16,32,128,128]{3,2,1,0:T(8,128)} async-done(((f32[1,32,128,128]{3,2,1,0:T(8,128)}), f32[16,32,128,128]{3,2,1,0:T(8,128)}) %all-gather.4.cloned.1.call-update) | async-done | bytes 33554448 | tf_op jit(solution)/shard_map/all_gather | solution.py:16
  194.2 3.2 while.19
  195.0 2.0 bitcast_add_fusion.6
  197.5 1.8 fusion.92
  199.3 0.9 copy-done.9
  200.3 10.7 %multiply_reduce_fusion.4 = (f32[256,2]{0,1:T(2,128)S(1)}, f32[256,2,16,128]{0,3,2,1:T(8,128)S(1)}, f32[256,2,16,128]{0,3,2,1:T(8,128)}) fusion(f32[256,2,16,128]{0,3,2,1:T(8,128)S(1)} %bitcast.222, bf16[256,2,16,128]{0,3,2,1:T(8,128)(2,1)S(1)} %bitcast.219, f32[2,16]{1,0:T(2,128)S(1)} %copy-done.38, f32[256,2,16]{0,2,1:T(8,128)S(1)} %copy-done.19, ...), kind=kOutput, calls=%fused_computation.59 | convolution fusion | flops 3244293632 | bytes 19564672 | tf_op jit(solution)/shard_map/jvp()/while/body/eval_jaxpr/gkts,sgkp->tgkp/dot_general | solution.py:36
  211.0 2.0 multiply_reduce_fusion.2
  213.1 2.1 fusion.33
  215.3 2.0 copy-done.2
  217.3 3.4 fusion.61
  220.8 1.2 dynamic-slice
  222.7 3.7 fusion.76
  226.4 12.8 %fusion.10 = (f32[2,16,256]{2,1,0:T(8,128)S(1)}, f32[2,16,256]{2,1,0:T(8,128)S(1)}, f32[2,16,256]{2,1,0:T(8,128)}, f32[2,256,256]{2,1,0:T(8,128)}) fusion(f32[2,16,256]{2,1,0:T(8,128)S(1)} %copy-done.24, f32[2,256,256]{2,1,0:T(8,128)} %fusion.95, f32[2,16,256]{2,1,0:T(8,128)S(1)} %copy-done.21, pred[256,256]{1,0:T(8,128)(4,1)S(1)} %iota_compare_fusion, ...), kind=kOutput, calls=%fused_computation.26 | convolution fusion | flops 3252527104 | bytes 7569408 | tf_op jit(solution)/shard_map/transpose(jvp())/while/body/eval_jaxpr/gkts,sgkp->tgkp/dot_general | solution.py:36
  241.8 1.3 mul.603
  244.0 5.5 copy.251
  249.5 8.5 %fusion.64 = f32[2,256,128]{2,1,0:T(8,128)S(1)} fusion(f32[2,16,128,128]{3,2,1,0:T(8,128)S(1)} %bitcast.212, f32[256,2,16,128]{0,3,2,1:T(8,128)} %copy-done.2, f32[256,2,16]{0,2,1:T(8,128)} %copy.242), kind=kOutput, calls=%fused_computation.84 | convolution fusion | flops 1611661312 | bytes 6586368 | tf_op jit(solution)/shard_map/transpose(jvp())/while/body/eval_jaxpr/tgn,gkpn->tgkp/dot_general | solution.py:37
  259.2 10.2 %all-reduce.3 = f32[4096]{0:T(1024)} all-reduce(f32[4096]{0:T(1024)} %bitcast.244), channel_id=2, replica_groups=mesh['ctx'=16,'tp'=4,'fsdp'=2] {'fsdp'}, use_global_device_ids=true, to_apply=%region_32.34.clone | all-reduce | flops 4096 | bytes 32768
  269.4 1.3 dynamic-slice.1
  270.7 65.2 %psum.31 = f32[2048]{0:T(1024)} all-reduce(f32[2048]{0:T(1024)} %dynamic-slice.1), channel_id=1, replica_groups=mesh['ctx'=16,'tp'=4,'fsdp'=2] {'ctx'}, use_global_device_ids=true, to_apply=%region_33.35 | all-reduce | flops 2048 | bytes 16384 | tf_op jit(solution)/shard_map/psum | solution.py:196
  336.0 1.3 broadcast_multiply_fusion.2
  337.3 10.1 %fusion.12 = (f32[32]{0:T(128)}, bf16[1,256,32,128]{3,2,1,0:T(8,128)(2,1)}) fusion(bf16[1,256,32,128]{3,2,1,0:T(8,128)(2,1)} %param.16, f32[1,256,32,128]{3,2,1,0:T(8,128)} %copy.251, bf16[1,256,32,128]{3,2,1,0:T(8,128)(2,1)} %param.17, bf16[1,256,32,128]{3,2,1,0:T(8,128)(2,1)} %param.26, f32[256,32]{1,0:T(8,128)S(1)} %copy.253, f32[256,32]{1,0:T(8,128)S(1)} %copy.252, ...), kind=kLoop, calls=%fused_computation.28 | loop fusion | flops 28311520 | bytes 12666112 | tf_op jit(solution)/shard_map/transpose(jvp())/reduce_sum | solution.py:78
  347.3 83.0 %all-gather.6.cloned.1.call-done = f32[16,32,128,128]{3,2,1,0:T(8,128)} async-done(((f32[1,32,128,128]{3,2,1,0:T(8,128)}), f32[16,32,128,128]{3,2,1,0:T(8,128)}) %all-gather.6.cloned.1.call-update) | async-done | bytes 33554448 | tf_op jit(solution)/shard_map/all_gather | solution.py:16
  430.3 1.6 broadcast.308
  431.9 63.6 %while.20 = (s32[]{:T(128)}, f32[32,128,128]{2,1,0:T(8,128)}, s32[]{:T(128)}, f32[16,32,128,128]{3,2,1,0:T(8,128)}, f32[16,32]{1,0:T(8,128)}, /*index=5*/s32[]{:T(128)}, s32[]{:T(128)}, s32[]{:T(128)}, s32[]{:T(128)}) while((s32[]{:T(128)}, f32[32,128,128]{2,1,0:T(8,128)}, s32[]{:T(128)}, f32[16,32,128,128]{3,2,1,0:T(8,128)}, ...), condition=%wide.region_9.11_spmd, body=%wide.region_8.10_spmd.sunk | while | flops 1048582 | bytes 6291987 | solution.py:25
  432.6 3.8 bitcast_add_fusion.7
  437.1 3.8 bitcast_add_fusion.7
  441.6 3.8 bitcast_add_fusion.7
  446.2 3.8 bitcast_add_fusion.7
  450.7 3.8 bitcast_add_fusion.7
  455.2 3.8 bitcast_add_fusion.7
  459.7 3.8 bitcast_add_fusion.7
  464.3 3.8 bitcast_add_fusion.7
  468.8 3.8 bitcast_add_fusion.7
  473.3 3.8 bitcast_add_fusion.7
  477.9 3.8 bitcast_add_fusion.7
  482.4 3.8 bitcast_add_fusion.7
  487.0 3.8 bitcast_add_fusion.7
  491.5 3.8 bitcast_add_fusion.7
  495.5 2.6 multiply_reduce_fusion.5
  498.8 7.1 %fusion.70 = f32[256,2,128]{0,2,1:T(8,128)} fusion(f32[2,16,128,128]{3,2,1,0:T(8,128)} %bitcast.213, bf16[256,2,16,128]{0,3,2,1:T(8,128)(2,1)} %bitcast.218, f32[256,2,16]{0,2,1:T(8,128)S(1)} %copy-done.18), kind=kOutput, calls=%fused_computation.90 | convolution fusion | flops 1612709888 | bytes 4489216 | tf_op jit(solution)/shard_map/transpose(jvp(gks,sgkp,sgn->gkpn))/dot_general | solution.py:90
  505.9 7.1 %fusion.21 = (f32[256,2,16]{0,2,1:T(8,128)}, f32[256,2,16]{0,2,1:T(8,128)S(1)}, f32[2,16,128,256]{3,2,1,0:T(8,128)}) fusion(bf16[256,2,16,128]{0,3,2,1:T(8,128)(2,1)S(1)} %bitcast.220, f32[2,16,128,256]{3,2,1,0:T(8,128)} %fusion.76, f32[2,16,128,128]{3,2,1,0:T(8,128)S(1)} %bitcast.214, bf16[256,2,128,1]{2,1,0,3:T(2,128)(2,1)S(1)} %bitcast.207), kind=kOutput, calls=%fused_computation.37 | convolution fusion | flops 1615839232 | bytes 12779520 | tf_op jit(solution)/shard_map/transpose(jvp(gks,sgkp,sgn->gkpn))/dot_general | solution.py:90
  514.4 3.7 fusion.113
  518.1 1.1 copy.260
  519.2 5.2 reduce-window.52
  525.5 1.0 copy.256
  529.5 1.8 pad_add_fusion
  531.3 1.0 copy.264
  532.4 5.0 reduce-window.54
  538.4 3.6 fusion.109
  543.6 68.8 %all-reduce.4 = (f32[32]{0:T(128)S(1)}, f32[32]{0:T(128)S(1)}, f32[32]{0:T(128)S(1)}) all-reduce(f32[32]{0:T(128)S(1)} %exponential_multiply_fusion.2, f32[32]{0:T(128)S(1)} %add.178, f32[32]{0:T(128)} %get-tuple-element.553), channel_id=1, replica_groups=mesh['ctx'=16,'tp'=4,'fsdp'=2] {'ctx','fsdp'}, use_global_device_ids=true, to_apply=%region_25.27 | all-reduce | flops 96 | bytes 768 | tf_op jit(solution)/shard_map/psum | solution.py:194
  612.9 1.0 copy.248
  614.0 2.6 fusion.69
  616.6 1.5 fusion.74
  619.7 13.8 %fusion.23 = bf16[256,2,16,128]{0,3,2,1:T(8,128)(2,1)S(1)} fusion(f32[2,16,128,256]{3,2,1,0:T(8,128)} %get-tuple-element.570, f32[2,16,128,256]{3,2,1,0:T(8,128)} %fusion.76, f32[256,2,16,128]{0,3,2,1:T(8,128)} %copy-done.2, f32[2,16,256]{2,1,0:T(8,128)} %copy.232, f32[2,256,256]{2,1,0:T(8,128)S(1)} %copy-done.16, f32[2,16,256]{2,1,0:T(8,128)} %copy-done.20, ...), kind=kOutput, calls=%fused_computation.40 | convolution fusion | flops 3239051264 | bytes 15401088 | tf_op jit(solution)/shard_map/transpose(jvp())/while/body/eval_jaxpr/gkts,sgkp->tgkp/dot_general | solution.py:36
  633.5 3.1 copy.278
  (164 shorter events, 35.9 us)
Async XLA Ops:
  7.2 8.6 %copy-start = (bf16[1,256,2,128]{3,2,1,0:T(2,128)(2,1)S(1)}, bf16[1,256,2,128]{3,2,1,0:T(2,128)(2,1)}, u32[]{:S(2)}) copy-start(bf16[1,256,2,128]{3,2,1,0:T(2,128)(2,1)} %param.19) | copy-start | bytes 393220
  7.2 186.8 %all-gather.4.cloned.1.call-start = ((), (), s32[]{:S(2)}) async-start(), calls=%async_computation | async-start | bytes 35651584 | tf_op jit(solution)/shard_map/all_gather | solution.py:16
  8.0 12.3 %copy-start.31 = (f32[2,16]{1,0:T(2,128)}, f32[2,16]{1,0:T(2,128)S(1)}, u32[]{:S(2)}) copy-start(f32[2,16]{1,0:T(2,128)S(1)} %neg.57) | copy-start | bytes 388
  9.6 1.9 copy-start.34
  11.9 0.5 copy-start.28
  12.8 6.6 %copy-start.17 = (f32[256,2,16]{0,2,1:T(8,128)}, f32[256,2,16]{0,2,1:T(8,128)S(1)}, u32[]{:S(2)}) copy-start(f32[256,2,16]{0,2,1:T(8,128)S(1)} %copy.238) | copy-start | bytes 98308
  15.8 7.7 %copy-start.5 = (bf16[1,256,32,128]{1,3,2,0:T(8,128)(2,1)}, bf16[1,256,32,128]{1,3,2,0:T(8,128)(2,1)S(1)}, u32[]{:S(2)}) copy-start(bf16[1,256,32,128]{1,3,2,0:T(8,128)(2,1)S(1)} %copy.233) | copy-start | bytes 6291460
  19.4 9.1 %copy-start.37 = (f32[32]{0:T(128)S(1)}, f32[32]{0:T(128)}, u32[]{:S(2)}) copy-start(f32[32]{0:T(128)} %param.23) | copy-start | bytes 388
  19.4 410.9 %all-gather.6.cloned.1.call-start = ((), (), s32[]{:S(2)}) async-start(), calls=%async_computation.1 | async-start | bytes 35651584 | tf_op jit(solution)/shard_map/all_gather | solution.py:16
  21.8 0.6 copy-start.20
  28.4 28.2 %copy-start.33 = (f32[2048]{0:T(1024)S(1)}, f32[2048]{0:T(1024)}, u32[]{:S(2)}) copy-start(f32[2048]{0:T(1024)} %param.24) | copy-start | bytes 24580
  28.4 34.5 %copy-start.11 = (bf16[1,256,2,128]{3,2,1,0:T(2,128)(2,1)S(1)}, bf16[1,256,2,128]{3,2,1,0:T(2,128)(2,1)}, u32[]{:S(2)}) copy-start(bf16[1,256,2,128]{3,2,1,0:T(2,128)(2,1)} %param.20) | copy-start | bytes 393220
  62.3 164.1 %copy-start.22 = (pred[256,256]{1,0:T(8,128)(4,1)}, pred[256,256]{1,0:T(8,128)(4,1)S(1)}, u32[]{:S(2)}) copy-start(pred[256,256]{1,0:T(8,128)(4,1)S(1)} %iota_compare_fusion) | copy-start | bytes 196612
  197.4 1.9 copy-start.6
  197.4 2.8 copy-start.9
  197.4 2.8 copy-start.19
  197.5 2.8 copy-start.21
  197.5 2.8 copy-start.23
  197.5 2.8 copy-start.38
  200.3 10.7 %copy-start.4 = (f32[1,256,32,128]{1,3,2,0:T(8,128)S(1)}, f32[1,256,32,128]{1,3,2,0:T(8,128)}, u32[]{:S(2)}) copy-start(f32[1,256,32,128]{1,3,2,0:T(8,128)} %copy.226) | copy-start | bytes 12582916
  200.3 10.7 %copy-start.30 = (f32[256]{0:T(256)S(1)}, f32[256]{0:T(256)}, u32[]{:S(2)}) copy-start(f32[256]{0:T(256)} %compare_convert_fusion) | copy-start | bytes 3076
  211.0 2.1 copy-start.25
  213.1 2.2 copy-start.26
  213.1 4.2 copy-start.36
  215.3 2.0 copy-start.2
  220.7 5.7 copy-start.24
  222.6 3.8 copy-start.3
  226.4 15.3 %copy-start.27 = (f32[256,2]{0,1:T(2,128)S(1)}, f32[256,2]{0,1:T(2,128)}, u32[]{:S(2)}) copy-start(f32[256,2]{0,1:T(2,128)} %copy-done.26) | copy-start | bytes 6148
  249.5 8.6 %copy-start.13 = (f32[2,256,256]{2,1,0:T(8,128)S(1)}, f32[2,256,256]{2,1,0:T(8,128)}, u32[]{:S(2)}) copy-start(f32[2,256,256]{2,1,0:T(8,128)} %get-tuple-element.509) | copy-start | bytes 1572868
  495.5 3.3 copy-start.18
  498.1 7.7 %copy-start.1 = (f32[32,128,128]{2,1,0:T(8,128)S(1)}, f32[32,128,128]{2,1,0:T(8,128)}, u32[]{:S(2)}) copy-start(f32[32,128,128]{2,1,0:T(8,128)} %get-tuple-element.450) | copy-start | bytes 6291460
  498.2 7.6 %copy-start.7 = (bf16[1,256,32,128]{1,3,2,0:T(8,128)(2,1)S(1)}, bf16[1,256,32,128]{1,3,2,0:T(8,128)(2,1)}, u32[]{:S(2)}) copy-start(bf16[1,256,32,128]{1,3,2,0:T(8,128)(2,1)} %copy-done.5) | copy-start | bytes 6291460
  505.9 8.5 %copy-start.29 = (f32[2,16]{1,0:T(2,128)S(1)}, f32[2,16]{1,0:T(2,128)}, u32[]{:S(2)}) copy-start(f32[2,16]{1,0:T(2,128)} %copy-done.28) | copy-start | bytes 388
  512.9 25.5 %copy-start.32 = (f32[2,16]{1,0:T(2,128)S(1)}, f32[2,16]{1,0:T(2,128)}, u32[]{:S(2)}) copy-start(f32[2,16]{1,0:T(2,128)} %copy-done.31) | copy-start | bytes 388
  512.9 25.5 %copy-start.35 = (f32[2,16]{1,0:T(2,128)S(1)}, f32[2,16]{1,0:T(2,128)}, u32[]{:S(2)}) copy-start(f32[2,16]{1,0:T(2,128)} %copy-done.34) | copy-start | bytes 388
  513.1 1.2 copy-start.10
  514.3 99.6 %copy-start.8 = (bf16[1,256,32,128]{1,3,2,0:T(8,128)(2,1)S(1)}, bf16[1,256,32,128]{1,3,2,0:T(8,128)(2,1)}, u32[]{:S(2)}) copy-start(bf16[1,256,32,128]{1,3,2,0:T(8,128)(2,1)} %copy-done.5) | copy-start | bytes 6291460
  518.1 98.5 %copy-start.12 = (bf16[1,256,2,128]{3,2,1,0:T(2,128)(2,1)S(1)}, bf16[1,256,2,128]{3,2,1,0:T(2,128)(2,1)}, u32[]{:S(2)}) copy-start(bf16[1,256,2,128]{3,2,1,0:T(2,128)(2,1)} %param.20) | copy-start | bytes 393220
  542.0 76.9 %copy-start.14 = (f32[2,16,256]{1,0,2:T(2,128)S(1)}, f32[2,16,256]{1,0,2:T(2,128)}, u32[]{:S(2)}) copy-start(f32[2,16,256]{1,0,2:T(2,128)} %get-tuple-element.542) | copy-start | bytes 98308
  542.0 76.9 %copy-start.15 = (f32[2,16,256]{1,0,2:T(2,128)S(1)}, f32[2,16,256]{1,0,2:T(2,128)}, u32[]{:S(2)}) copy-start(f32[2,16,256]{1,0,2:T(2,128)} %get-tuple-element.556) | copy-start | bytes 98308
  542.0 77.7 %copy-start.16 = (f32[2,256,256]{2,1,0:T(8,128)S(1)}, f32[2,256,256]{2,1,0:T(8,128)}, u32[]{:S(2)}) copy-start(f32[2,256,256]{2,1,0:T(8,128)} %fusion.95) | copy-start | bytes 1572868
Sparse Core Ops, SparseCore 0:
  19.5 174.4 all-gather.3
  220.9 209.3 all-gather.5
where the time goes:
time: 652 us; the launch traced here: 644 us
  waiting for transfers between devices  213 us (33%)
  blocking collectives  171 us (26%)
  other arithmetic  104 us (16%)
  matrix products  77.9 us (12%)
  local copies, waits for them, and re-layouts  61.6 us (9%)
  between operations  16.3 us (2%)
    all_gather x2, waiting for transfers between devices, prefix(): gathered = jax.tree.map(lambda a: lax.all_gather(a, axis), part)  213 us
    psum x1, blocking collectives, per_device(): head_totals = lax.psum((grad_a, grad_bias, grad_skip), ('ctx', 'fsdp'))  68.8 us
    psum x1, blocking collectives, per_device(): gain_total = lax.psum(gain_part, 'ctx')  65.2 us
    add x15, other arithmetic, join_states(): later[1] + jnp.exp(later[0])[..., None, None] * earlier[1]  55.8 us
    dot_general x3, matrix products, block_step(): output = jnp.einsum('gkts,sgkp->tgkp', weights, x_block, precision=HIGH)  37.2 us
    all_gather x1, blocking collectives, prefix(): gathered = jax.tree.map(lambda a: lax.all_gather(a, axis), part)  21.7 us
    dot_general x3, matrix products, local_states(): jnp.einsum('gks,sgkp,sgn->gkpn', weighting, x_all, b_all, precision=HIGH)  17.6 us
    unnamed x85, local copies, waits for them, and re-layouts  14.5 us
  transfers between devices with their start and end apart: 2, of which 2 were waited for; matrix products, arithmetic and copies ran while one was open for 10% of the time, Pallas kernels for 0%

commit v1 on v0

v1 whole, which is shorter than its diff:
```python
import functools
import math

import jax
import jax.numpy as jnp
from jax import lax
from jax.experimental import pallas as pl
from jax.experimental.pallas import tpu as pltpu
from jax.sharding import PartitionSpec as P

EPS = 1e-05
HIGH = lax.Precision.HIGHEST
F32 = jnp.float32
BF16 = jnp.bfloat16
MESH = pl.DeviceIdType.MESH
VMEM_LIMIT = 48 * 1024 * 1024


def split(value):
    high = value.astype(BF16)
    return high, (value - high.astype(F32)).astype(BF16)


def dot(left, right):
    return jnp.dot(left, right, preferred_element_type=F32)


def dot_nt(left, right):
    return lax.dot_general(left, right, (((1,), (1,)), ((), ())), preferred_element_type=F32)


def dot_tn(left, right):
    return lax.dot_general(left, right, (((0,), (0,)), ((), ())), preferred_element_type=F32)


def softplus(value):
    return jnp.maximum(value, 0.0) + jnp.log1p(jnp.exp(-jnp.abs(value)))


def sigmoid(value):
    return 1.0 / (1.0 + jnp.exp(-value))


def lower(length):
    row = lax.broadcasted_iota(jnp.int32, (length, length), 0)
    column = lax.broadcasted_iota(jnp.int32, (length, length), 1)
    return row >= column


def local_kernel(x_ref, dt_ref, a_ref, bias_ref, bt_ref, xh_ref, er_ref, es_ref, ec_ref, fresh_ref, wide):
    tokens, heads, dim = x_ref.shape
    wide[...] = x_ref[...].astype(F32).reshape(tokens * heads, dim)
    step = softplus(dt_ref[...].astype(F32) + bias_ref[...])
    log_step = step * (-jnp.exp(a_ref[...]))
    upto = jnp.where(lower(tokens), 1.0, 0.0).astype(F32)
    running = lax.dot_general(
        log_step, upto, (((1,), (1,)), ((), ())), precision=HIGH, preferred_element_type=F32
    )
    half = 0.5 * running[:, tokens - 1 :]
    er_ref[0] = jnp.transpose(jnp.exp(running - half))
    es = jnp.transpose(jnp.exp(half - running) * step)
    es_ref[0] = es
    ec_ref[...] = jnp.broadcast_to(jnp.exp(half), ec_ref.shape)
    for head in range(0, heads, 2):
        scaled = []
        for one in (head, head + 1):
            x_one = wide[pl.ds(one, tokens, stride=heads), :]
            xh_ref[:, one * dim : (one + 1) * dim] = x_one.astype(BF16)
            scaled.append(x_one * es[:, one : one + 1])
        high, low = split(jnp.concatenate(scaled, axis=1))
        state = dot(bt_ref[0], high) + dot(bt_ref[0], low)
        for at, one in enumerate((head, head + 1)):
            fresh_ref[one] = state[:, at * dim : (at + 1) * dim] * ec_ref[one : one + 1, :]


def chain_kernel(
    backward, exchange, fresh_ref, ec_ref, gain_ref, carried_ref, final_ref, gains_ref, send_sem, recv_sem, gain_sem
):
    count = lax.axis_size("ctx")
    me = lax.axis_index("ctx")
    pieces = fresh_ref.shape[0]
    right, left = lax.rem(me + 1, count), lax.rem(me + count - 1, count)
    target = left if backward else right
    place = count - 1 - me if backward else me
    mine = lax.axis_index("fsdp")
    other = 1 - mine
    barrier = pltpu.get_barrier_semaphore()
    for neighbour in (left, right):
        pl.semaphore_signal(barrier, inc=1, device_id={"ctx": neighbour}, device_id_type=MESH)
    if exchange:
        pl.semaphore_signal(barrier, inc=1, device_id={"fsdp": other}, device_id_type=MESH)
    pl.semaphore_wait(barrier, 3 if exchange else 2)

    def piece_copy(at):
        return pltpu.make_async_remote_copy(
            src_ref=final_ref.at[at],
            dst_ref=carried_ref.at[at],
            send_sem=send_sem.at[at],
            recv_sem=recv_sem.at[at],
            device_id={"ctx": target},
            device_id_type=MESH,
        )

    if exchange:
        gains_ref[mine] = gain_ref[...]
        gain_copy = pltpu.make_async_remote_copy(
            src_ref=gain_ref,
            dst_ref=gains_ref.at[mine],
            send_sem=gain_sem.at[0],
            recv_sem=gain_sem.at[1],
            device_id={"fsdp": other},
            device_id_type=MESH,
        )
        gain_copy.start()

    @pl.when(place == 0)
    def _():
        carried_ref[...] = jnp.zeros_like(carried_ref)

    def one(at, carry):
        @pl.when(place > 0)
        def _():
            piece_copy(at).wait_recv()

        decay = ec_ref[pl.ds(at, 1), :]
        final_ref[at] = fresh_ref[at] + (decay * decay) * carried_ref[at]

        @pl.when(place < count - 1)
        def _():
            piece_copy(at).start()

        return carry

    lax.fori_loop(0, pieces, one, 0)

    @pl.when(place < count - 1)
    def _():
        def done(at, carry):
            piece_copy(at).wait_send()
            return carry

        lax.fori_loop(0, pieces, done, 0)

    if exchange:
        gain_copy.wait()


def mixer_kernel(
    limit_ref,
    xh_ref,
    gate_ref,
    out_ref,
    er_ref,
    es_ref,
    ec_ref,
    skip_ref,
    gain_ref,
    state_ref,
    b_ref,
    bt_ref,
    c_ref,
    ct_ref,
    ggate_ref,
    gx_ref,
    local_ref,
    ggain_ref,
    gskip_ref,
    rho_ref,
    sigma_ref,
    gc_ref,
    gb_ref,
    wide_gate,
    wide_out,
    mixed,
):
    tokens, heads, dim = gate_ref.shape
    wide_gate[...] = gate_ref[...].astype(F32).reshape(tokens * heads, dim)
    keep = lax.broadcasted_iota(jnp.int32, (tokens, 1, 1), 0) < limit_ref[0]
    wide_out[...] = jnp.where(keep, out_ref[...].astype(F32), 0.0).reshape(tokens * heads, dim)
    er, es = er_ref[0], es_ref[0]
    causal = lower(tokens)
    scores = jnp.where(causal, dot(c_ref[0], bt_ref[0]), 0.0)
    m_high, m_low = split(scores)
    scores_t = jnp.transpose(scores)
    mt_high, mt_low = split(scores_t)

    def scaled_pair(head):
        return jnp.concatenate(
            [
                xh_ref[:, one * dim : (one + 1) * dim].astype(F32) * es[:, one : one + 1]
                for one in (head, head + 1)
            ],
            axis=1,
        )

    def state_pair(head):
        return jnp.concatenate(
            [state_ref[one] * ec_ref[one : one + 1, :] for one in (head, head + 1)], axis=1
        )

    square = jnp.zeros((tokens, dim), F32)
    cross = jnp.zeros((tokens, dim), F32)
    for head in range(0, heads, 2):
        x_high, x_low = split(scaled_pair(head))
        s_high, s_low = split(state_pair(head))
        scanned = dot(m_high, x_high) + dot(m_high, x_low) + dot(m_low, x_high)
        scanned = scanned + dot(c_ref[0], s_high) + dot(c_ref[0], s_low)
        for at, one in enumerate((head, head + 1)):
            x_one = xh_ref[:, one * dim : (one + 1) * dim].astype(F32)
            mix = scanned[:, at * dim : (at + 1) * dim] * er[:, one : one + 1]
            mix = mix + x_one * skip_ref[one : one + 1, :]
            mixed[:, one * dim : (one + 1) * dim] = mix
            gate = wide_gate[pl.ds(one, tokens, stride=heads), :]
            gated = mix * gate * sigmoid(gate)
            upper = wide_out[pl.ds(one, tokens, stride=heads), :] * gain_ref[one : one + 1, :]
            square = square + gated * gated
            cross = cross + upper * gated
    width = heads * dim
    inverse = lax.rsqrt(jnp.sum(square, axis=1, keepdims=True) * (1.0 / width) + EPS)
    pull = inverse * inverse * inverse * (jnp.sum(cross, axis=1, keepdims=True) * (1.0 / width))
    lane = lax.broadcasted_iota(jnp.int32, (tokens, heads), 1)
    rho = jnp.zeros((tokens, heads), F32)
    sigma = jnp.zeros((tokens, heads), F32)
    grad_m = jnp.zeros((tokens, tokens), F32)
    grad_c = jnp.zeros((tokens, dim), F32)
    for head in range(0, heads, 2):
        scaled, grads = [], []
        for one in (head, head + 1):
            gate = wide_gate[pl.ds(one, tokens, stride=heads), :]
            sig = sigmoid(gate)
            silu = gate * sig
            mix = mixed[:, one * dim : (one + 1) * dim]
            gated = mix * silu
            cot = wide_out[pl.ds(one, tokens, stride=heads), :]
            gain_row = gain_ref[one : one + 1, :]
            ggain_ref[one : one + 1, :] = jnp.sum(cot * gated * inverse, axis=0, keepdims=True)
            grad_gated = inverse * (cot * gain_row) - pull * gated
            grad_mix = grad_gated * silu
            wide_gate[pl.ds(one, tokens, stride=heads), :] = (
                grad_gated * mix * (sig + silu * (1.0 - sig))
            )
            x_one = xh_ref[:, one * dim : (one + 1) * dim].astype(F32)
            skip_x = x_one * skip_ref[one : one + 1, :]
            gskip_ref[one : one + 1, :] = jnp.sum(grad_mix * x_one, axis=0, keepdims=True)
            gx_ref[:, one * dim : (one + 1) * dim] = grad_mix * skip_ref[one : one + 1, :]
            rho = jnp.where(
                lane == one, jnp.sum(grad_mix * (mix - skip_x), axis=1, keepdims=True), rho
            )
            grads.append(grad_mix * er[:, one : one + 1])
        y_high, y_low = split(jnp.concatenate(grads, axis=1))
        back = dot(ct_ref[0], y_high) + dot(ct_ref[0], y_low)
        x_high, x_low = split(scaled_pair(head))
        s_high, s_low = split(state_pair(head))
        grad_m = grad_m + dot_nt(y_high, x_high) + dot_nt(y_high, x_low) + dot_nt(y_low, x_high)
        grad_c = grad_c + dot_nt(y_high, s_high) + dot_nt(y_high, s_low) + dot_nt(y_low, s_high)
        grad_scaled = dot(mt_high, y_high) + dot(mt_high, y_low) + dot(mt_low, y_high)
        for at, one in enumerate((head, head + 1)):
            local_ref[one] = back[:, at * dim : (at + 1) * dim] * ec_ref[one : one + 1, :]
            inner = grad_scaled[:, at * dim : (at + 1) * dim] * es[:, one : one + 1]
            x_one = xh_ref[:, one * dim : (one + 1) * dim].astype(F32)
            sigma = jnp.where(lane == one, jnp.sum(inner * x_one, axis=1, keepdims=True), sigma)
            gx_ref[:, one * dim : (one + 1) * dim] += inner
    ggate_ref[...] = wide_gate[...].reshape(tokens, heads, dim).astype(BF16)
    rho_ref[0] = rho
    sigma_ref[0] = sigma
    grad_m = jnp.where(causal, grad_m, 0.0)
    g_high, g_low = split(grad_m)
    gc_ref[0] = (grad_c + dot(g_high, b_ref[0]) + dot(g_low, b_ref[0])).astype(BF16)
    t_high, t_low = split(jnp.transpose(grad_m))
    gb_ref[0] = dot(t_high, c_ref[0]) + dot(t_low, c_ref[0])


def final_kernel(
    xh_ref,
    es_ref,
    ec_ref,
    behind_ref,
    end_ref,
    b_ref,
    gx_ref,
    gb_ref,
    rho_ref,
    sigma_ref,
    gskip_ref,
    dt_ref,
    a_ref,
    bias_ref,
    gx_out,
    gb_out,
    gdt_out,
    small_out,
    wide,
    rows,
):
    tokens, heads, dim = gx_out.shape
    es = es_ref[0]
    lane = lax.broadcasted_iota(jnp.int32, (tokens, heads), 1)
    sigma = jnp.zeros((tokens, heads), F32)
    grad_b = gb_ref[0]
    for head in range(0, heads, 2):
        scaled, states = [], []
        for one in (head, head + 1):
            scaled.append(
                xh_ref[:, one * dim : (one + 1) * dim].astype(F32) * es[:, one : one + 1]
            )
            states.append(behind_ref[one] * ec_ref[one : one + 1, :])
            rows[one : one + 1, :] = jnp.sum(behind_ref[one] * end_ref[one], axis=0, keepdims=True)
        x_high, x_low = split(jnp.concatenate(scaled, axis=1))
        s_high, s_low = split(jnp.concatenate(states, axis=1))
        grad_b = grad_b + dot_nt(x_high, s_high) + dot_nt(x_high, s_low) + dot_nt(x_low, s_high)
        grad_scaled = dot(b_ref[0], s_high) + dot(b_ref[0], s_low)
        for at, one in enumerate((head, head + 1)):
            inner = grad_scaled[:, at * dim : (at + 1) * dim] * es[:, one : one + 1]
            x_one = xh_ref[:, one * dim : (one + 1) * dim].astype(F32)
            sigma = jnp.where(lane == one, jnp.sum(inner * x_one, axis=1, keepdims=True), sigma)
            wide[pl.ds(one, tokens, stride=heads), :] = (
                gx_ref[:, one * dim : (one + 1) * dim] + inner
            )
    gx_out[...] = wide[...].reshape(tokens, heads, dim).astype(BF16)
    gb_out[0] = grad_b.astype(BF16)
    sigma = sigma + sigma_ref[0]
    after = jnp.where(lower(tokens), 1.0, 0.0).astype(F32)
    sums = lax.dot_general(
        rho_ref[0] - sigma, after, (((0,), (0,)), ((), ())), precision=HIGH, preferred_element_type=F32
    )
    sigma_t = jnp.transpose(sigma)
    grad_log = sums + jnp.sum(rows[...], axis=1, keepdims=True)
    value = dt_ref[...].astype(F32) + bias_ref[...]
    step = softplus(value)
    rate = -jnp.exp(a_ref[...])
    grad_dt = (sigma_t / step + grad_log * rate) * sigmoid(value)
    gdt_out[...] = grad_dt.astype(BF16)
    grad_a = jnp.sum(grad_log * step, axis=1, keepdims=True) * rate
    grad_bias = jnp.sum(grad_dt, axis=1, keepdims=True)
    grad_skip = jnp.sum(gskip_ref[...], axis=1, keepdims=True)
    place = lax.broadcasted_iota(jnp.int32, small_out.shape, 1)
    small_out[...] = jnp.where(
        place == 0, grad_a, jnp.where(place == 1, grad_bias, jnp.where(place == 2, grad_skip, 0.0))
    )


def reduce_kernel(
    scale, gain_ref, small_ref, gain_out, small_out, first, gathered, first_sem, send_sem, recv_sem
):
    count = lax.axis_size("ctx")
    me = lax.axis_index("ctx")
    mine = lax.axis_index("fsdp")
    other = 1 - mine
    half = gain_out.shape[0]
    barrier = pltpu.get_barrier_semaphore()
    pl.semaphore_signal(barrier, inc=1, device_id={"fsdp": other}, device_id_type=MESH)
    for hop in range(1, count):
        pl.semaphore_signal(
            barrier, inc=1, device_id={"ctx": lax.rem(me + hop, count)}, device_id_type=MESH
        )
    pl.semaphore_wait(barrier, count)
    first[0, :half] = gain_ref[pl.ds(pl.multiple_of(other * half, half), half), :]
    first[0, half:] = small_ref[...]
    swap = pltpu.make_async_remote_copy(
        src_ref=first.at[0],
        dst_ref=first.at[1],
        send_sem=first_sem.at[0],
        recv_sem=first_sem.at[1],
        device_id={"fsdp": other},
        device_id_type=MESH,
    )
    swap.start()
    swap.wait()
    gathered[0, :half] = first[1, :half] + gain_ref[pl.ds(pl.multiple_of(mine * half, half), half), :]
    gathered[0, half:] = first[1, half:] + small_ref[...]

    def piece_copy(hop):
        return pltpu.make_async_remote_copy(
            src_ref=gathered.at[0],
            dst_ref=gathered.at[hop],
            send_sem=send_sem.at[hop],
            recv_sem=recv_sem.at[hop],
            device_id={"ctx": lax.rem(me + hop, count)},
            device_id_type=MESH,
        )

    for hop in range(1, count):
        piece_copy(hop).start()
    for hop in range(1, count):
        piece_copy(hop).wait()
    total = gathered[0]
    for hop in range(1, count):
        total = total + gathered[hop]
    gain_out[...] = total[:half] * scale
    small_out[...] = total[half:] * scale


def per_device(
    x_input,
    gate_input,
    dt_raw,
    b_input,
    c_input,
    a_log,
    dt_bias,
    skip_weight,
    norm_gain,
    valid_len,
    grad_output,
):
    _, tokens, heads, dim = x_input.shape
    groups, state = b_input.shape[2:]
    per_group = heads // groups
    count = lax.axis_size("ctx")
    width = per_group * dim
    shape = jax.ShapeDtypeStruct
    whole = pl.BlockSpec(memory_space=pltpu.VMEM)

    def params(**extra):
        return pltpu.CompilerParams(vmem_limit_bytes=VMEM_LIMIT, **extra)

    natural = pl.BlockSpec((tokens, per_group, dim), lambda g: (0, g, 0))
    flat = pl.BlockSpec((tokens, width), lambda g: (0, g))
    times = pl.BlockSpec((per_group, tokens), lambda g: (g, 0))
    column = pl.BlockSpec((per_group, 1), lambda g: (g, 0))
    line = pl.BlockSpec((per_group, dim), lambda g: (g, 0))
    states = pl.BlockSpec((per_group, state, dim), lambda g: (g, 0, 0))
    token_head = pl.BlockSpec((1, tokens, per_group), lambda g: (g, 0, 0))
    tall = pl.BlockSpec((1, tokens, state), lambda g: (g, 0, 0))
    broad = pl.BlockSpec((1, state, tokens), lambda g: (g, 0, 0))

    b_tall = jnp.transpose(b_input[0], (1, 0, 2))
    c_tall = jnp.transpose(c_input[0], (1, 0, 2))
    b_broad = jnp.transpose(b_input[0], (1, 2, 0))
    c_broad = jnp.transpose(c_input[0], (1, 2, 0))
    a_column = a_log[:, None]
    bias_column = dt_bias[:, None]
    skip_line = jnp.broadcast_to(skip_weight[:, None], (heads, dim))
    limit = valid_len - lax.axis_index("ctx") * tokens

    xh, er, es, ec, fresh = pl.pallas_call(
        local_kernel,
        grid=(groups,),
        in_specs=[natural, times, column, column, broad],
        out_specs=[flat, token_head, token_head, line, states],
        out_shape=[
            shape((tokens, heads * dim), BF16),
            shape((groups, tokens, per_group), F32),
            shape((groups, tokens, per_group), F32),
            shape((heads, dim), F32),
            shape((heads, state, dim), F32),
        ],
        scratch_shapes=[pltpu.VMEM((tokens * per_group, dim), F32)],
        compiler_params=params(),
        name="local_states",
    )(x_input[0], dt_raw[0], a_column, bias_column, b_broad)

    def chain(backward, fresh_states, gain):
        return pl.pallas_call(
            functools.partial(chain_kernel, backward, not backward),
            in_specs=[whole] * 3,
            out_specs=[whole] * 3,
            out_shape=[
                shape((heads, state, dim), F32),
                shape((heads, state, dim), F32),
                shape((2, heads // 2, dim), F32),
            ],
            scratch_shapes=[
                pltpu.SemaphoreType.DMA((heads,)),
                pltpu.SemaphoreType.DMA((heads,)),
                pltpu.SemaphoreType.DMA((2,)),
            ],
            compiler_params=params(collective_id=1 if backward else 0, has_side_effects=True),
            name="chain_backward" if backward else "chain_forward",
        )(fresh_states, ec, gain)

    own_gain = norm_gain.reshape(heads // 2, dim)
    carried, ends, gains = chain(False, fresh, own_gain)

    ggate, gx_part, local, ggain, gskip, rho, sigma, grad_c, gb_part = pl.pallas_call(
        mixer_kernel,
        grid=(groups,),
        in_specs=[
            pl.BlockSpec(memory_space=pltpu.SMEM),
            flat,
            natural,
            natural,
            token_head,
            token_head,
            line,
            line,
            line,
            states,
            tall,
            broad,
            tall,
            broad,
        ],
        out_specs=[natural, flat, states, line, line, token_head, token_head, tall, tall],
        out_shape=[
            shape((tokens, heads, dim), BF16),
            shape((tokens, heads * dim), F32),
            shape((heads, state, dim), F32),
            shape((heads, dim), F32),
            shape((heads, dim), F32),
            shape((groups, tokens, per_group), F32),
            shape((groups, tokens, per_group), F32),
            shape((groups, tokens, state), BF16),
            shape((groups, tokens, state), F32),
        ],
        scratch_shapes=[
            pltpu.VMEM((tokens * per_group, dim), F32),
            pltpu.VMEM((tokens * per_group, dim), F32),
            pltpu.VMEM((tokens, width), F32),
        ],
        compiler_params=params(),
        name="mixer",
    )(
        limit,
        xh,
        gate_input[0],
        grad_output[0],
        er,
        es,
        ec,
        skip_line,
        gains.reshape(heads, dim),
        carried,
        b_tall,
        b_broad,
        c_tall,
        c_broad,
    )

    behind, _, _ = chain(True, local, own_gain)

    grad_x, grad_b, grad_dt, small = pl.pallas_call(
        final_kernel,
        grid=(groups,),
        in_specs=[
            flat,
            token_head,
            line,
            states,
            states,
            tall,
            flat,
            tall,
            token_head,
            token_head,
            line,
            times,
            column,
            column,
        ],
        out_specs=[natural, tall, times, line],
        out_shape=[
            shape((tokens, heads, dim), BF16),
            shape((groups, tokens, state), BF16),
            shape((heads, tokens), BF16),
            shape((heads, dim), F32),
        ],
        scratch_shapes=[
            pltpu.VMEM((tokens * per_group, dim), F32),
            pltpu.VMEM((per_group, dim), F32),
        ],
        compiler_params=params(),
        name="final",
    )(
        xh,
        es,
        ec,
        behind,
        ends,
        b_tall,
        gx_part,
        gb_part,
        rho,
        sigma,
        gskip,
        dt_raw[0],
        a_column,
        bias_column,
    )

    scale = 1.0 / math.sqrt(tokens * count * lax.axis_size("fsdp"))
    rows = heads // 2 + heads
    gain_total, small_total = pl.pallas_call(
        functools.partial(reduce_kernel, scale),
        in_specs=[whole] * 2,
        out_specs=[whole] * 2,
        out_shape=[shape((heads // 2, dim), F32), shape((heads, dim), F32)],
        scratch_shapes=[
            pltpu.VMEM((2, rows, dim), F32),
            pltpu.VMEM((count, rows, dim), F32),
            pltpu.SemaphoreType.DMA((2,)),
            pltpu.SemaphoreType.DMA((count,)),
            pltpu.SemaphoreType.DMA((count,)),
        ],
        compiler_params=params(collective_id=2, has_side_effects=True),
        name="reduce_small",
    )(ggain, small)

    return (
        grad_x[None],
        ggate[None],
        grad_dt[None],
        jnp.transpose(grad_b, (1, 0, 2))[None],
        jnp.transpose(grad_c, (1, 0, 2))[None],
        small_total[:, 0],
        small_total[:, 1],
        small_total[:, 2],
        gain_total.reshape(heads // 2 * dim),
    )


def solution(mesh):
    placed = (
        P("fsdp", "ctx", "tp", None),
        P("fsdp", "ctx", "tp", None),
        P("fsdp", "tp", "ctx"),
        P("fsdp", "ctx", "tp", None),
        P("fsdp", "ctx", "tp", None),
        P("tp"),
        P("tp"),
        P("tp"),
        P(("tp", "fsdp")),
        P("fsdp"),
        P("fsdp", "ctx", "tp", None),
    )
    return jax.shard_map(
        per_device,
        mesh=mesh,
        in_specs=placed,
        out_specs=(
            P("fsdp", "ctx", "tp", None),
            P("fsdp", "ctx", "tp", None),
            P("fsdp", "tp", "ctx"),
            P("fsdp", "ctx", "tp", None),
            P("fsdp", "ctx", "tp", None),
            P("tp"),
            P("tp"),
            P("tp"),
            P(("tp", "fsdp")),
        ),
        check_vma=False,
    )
```

time: 652 us -> 180 us (0.28); the launches traced: 644 us -> 180 us
  waiting for transfers between devices: 213 us -> 0 us
  blocking collectives: 171 us -> 0 us
  Pallas kernels: 0 us -> 163 us
  other arithmetic: 104 us -> 0 us
  matrix products: 77.9 us -> 0 us
  local copies, waits for them, and re-layouts: 61.6 us -> 15.5 us
  between operations: 16.3 us -> 1.4 us
    all_gather x2 -> x0, waiting for transfers between devices: 213 us -> none  [prefix(): gathered = jax.tree.map(lambda a: lax.all_gather(a, axis), part)]
    pallas_call x0 -> x6, Pallas kernels: none -> 163 us  [the longest x2 113 us: chain(): pl.pallas_call(functools.partial(chain_kernel, backward, not backward), i...]
    psum x2 -> x0, blocking collectives: 134 us -> none  [the longest x1 68.8 us: per_device(): head_totals = lax.psum((grad_a, grad_bias, grad_skip), ('ctx', 'fsdp'))]
    dot_general x14 -> x0, matrix products: 77.9 us -> none  [the longest x3 37.2 us: block_step(): output = jnp.einsum('gkts,sgkp->tgkp', weights, x_block, precision=HIGH)]
    add x17 -> x0, other arithmetic: 56.5 us -> none  [the longest x15 55.8 us: join_states(): later[1] + jnp.exp(later[0])[..., None, None] * earlier[1]]
    all_gather x2 -> x0, blocking collectives: 26.8 us -> none  [the longest x1 21.7 us: prefix(): gathered = jax.tree.map(lambda a: lax.all_gather(a, axis), part)]
    reduce_sum x7 -> x0, other arithmetic: 24.4 us -> none  [the longest x1 10.1 us: mixer_forward(): mixed = scanned + skip_weight[None, :, :, None] * x_all]
    another operation x12 -> x0, other arithmetic: 12.9 us -> none
  transfers between devices with their start and end apart: 2 -> 0, of which waited for: 2 -> 0; matrix products, arithmetic and copies ran while one was open for 10% -> 0% of each run, Pallas kernels for 0% -> 0%
where the time goes in v1:
time: 180 us
  Pallas kernels  163 us (91%)
  local copies, waits for them, and re-layouts  15.5 us (9%)
    pallas_call x2, Pallas kernels, chain(): pl.pallas_call(functools.partial(chain_kernel, backward, not backward), i...  113 us
    pallas_call x1, Pallas kernels, per_device(): pl.pallas_call(mixer_kernel, grid=(groups,), in_specs=[pl.BlockSpec(memor...  22.2 us
    pallas_call x1, Pallas kernels, per_device(): pl.pallas_call(functools.partial(reduce_kernel, scale), in_specs=[whole]...  13.4 us
    unnamed x20, local copies, waits for them, and re-layouts  10.6 us
    pallas_call x1, Pallas kernels, per_device(): pl.pallas_call(final_kernel, grid=(groups,), in_specs=[flat, token_head,...  8.75 us
    pallas_call x1, Pallas kernels, per_device(): pl.pallas_call(local_kernel, grid=(groups,), in_specs=[natural, times, co...  5.7 us

profile of v1, /device:TPU:1, one launch (start us, length us, event | category | flops | bytes accessed | tf_op | source)
XLA Modules:
  0.0 179.6 jit_solution(1468366780241192046)
XLA Ops:
  0.6 0.0 copy-start.7
  1.3 0.7 copy.32.a_ref
  2.0 0.7 copy.33.bias_ref
  2.8 0.7 broadcast_in_dim.29.skip_ref
  3.5 1.0 copy.42
  4.5 1.0 copy.35
  5.6 1.0 copy_bitcast_fusion
  6.6 0.0 copy-start.6
  6.6 0.7 copy-done.6
  7.3 5.7 %local_states.1 = (bf16[256,4096]{1,0:T(8,128)(2,1)S(1)}, f32[2,256,16]{2,1,0:T(8,128)S(1)}, f32[2,256,16]{2,1,0:T(8,128)S(1)}, f32[32,128]{1,0:T(8,128)S(1)}, f32[32,128,128]{2,1,0:T(8,128)S(1)}) custom-call(bf16[256,32,128]{2,1,0:T(8,128)(2,1)} %bitcast.44, bf16[32,256]{1,0:T(8,128)(2,1)S(1)} %bitcast.36, f32[32,1]{1,0:T(8,128)S(1)} %copy.32.a_ref, ...), custom_call_target="tpu_custom_call" | custom-call | tf_op jit(solution)/shard_map/local_states/pallas_call | solution.py:436
  13.0 0.0 copy-start
  13.0 1.3 copy-done
  14.3 0.0 copy-start.4
  14.3 1.3 copy-done.4
  15.6 0.0 copy-done.7
  15.6 31.5 %chain_forward.1 = (f32[32,128,128]{2,1,0:T(8,128)S(1)}, f32[32,128,128]{2,1,0:T(8,128)S(1)}, f32[2,16,128]{2,1,0:T(8,128)S(1)}) custom-call(f32[32,128,128]{2,1,0:T(8,128)} %copy-done.4, f32[32,128]{1,0:T(8,128)S(1)} %get-tuple-element.35.ec_ref, f32[16,128]{1,0:T(8,128)S(1)} %bitcast.38), custom_call_target="tpu_custom_call" | custom-call | tf_op jit(solution)/shard_map/chain_forward/pallas_call | solution.py:454
  47.1 0.0 copy-start.2
  47.1 1.4 copy-done.2
  48.5 0.0 copy-start.5
  48.5 1.3 copy-done.5
  49.8 22.2 %mixer.1 = (bf16[256,32,128]{2,1,0:T(8,128)(2,1)}, f32[256,4096]{1,0:T(8,128)}, f32[32,128,128]{2,1,0:T(8,128)S(1)}, f32[32,128]{1,0:T(8,128)S(1)}, f32[32,128]{...) custom-call(s32[1]{0:T(128)S(6)} %sub.7.limit_ref, ...), custom_call_target="tpu_custom_call" | custom-call | tf_op jit(solution)/shard_map/mixer/pallas_call | solution.py:475
  71.9 0.0 copy-start.3
  71.9 1.4 copy-done.3
  73.3 0.0 copy-start.1
  73.3 0.8 copy.41
  74.1 81.2 %chain_backward.1 = (f32[32,128,128]{2,1,0:T(8,128)S(1)}, f32[32,128,128]{2,1,0:T(8,128)}, f32[2,16,128]{2,1,0:T(8,128)}) custom-call(f32[32,128,128]{2,1,0:T(8,128)} %copy-done.3, f32[32,128]{1,0:T(8,128)S(1)} %get-tuple-element.35.ec_ref, f32[16,128]{1,0:T(8,128)S(1)} %bitcast.39), custom_call_target="tpu_custom_call" | custom-call | tf_op jit(solution)/shard_map/chain_backward/pallas_call | solution.py:454
  155.3 0.0 copy-done.1
  155.3 8.8 %final.1 = (bf16[256,32,128]{2,1,0:T(8,128)(2,1)}, bf16[2,256,128]{2,1,0:T(8,128)(2,1)S(1)}, bf16[32,256]{1,0:T(8,128)(2,1)}, f32[32,128]{1,0:T(8,128)S(1)}) custom-call(bf16[256,4096]{1,0:T(8,128)(2,1)S(1)} %copy-done.1, f32[2,256,16]{2,1,0:T(8,128)S(1)} %get-tuple-element.34.es_ref, f32[32,128]{1,0:T(8,128)S(1)} %get-tuple-element.35.ec_ref, ...), custom_call_target="tpu_custom_call" | custom-call | tf_op jit(solution)/shard_map/final/pallas_call | solution.py:532
  164.1 13.4 %reduce_small.1 = (f32[16,128]{1,0:T(8,128)S(1)}, f32[32,128]{1,0:T(8,128)S(1)}) custom-call(f32[32,128]{1,0:T(8,128)S(1)} %get-tuple-element.53.gain_ref, f32[32,128]{1,0:T(8,128)S(1)} %get-tuple-element.54.small_ref), custom_call_target="tpu_custom_call" | custom-call | tf_op jit(solution)/shard_map/reduce_small/pallas_call | solution.py:583
  177.5 0.7 slice_reduce_fusion
  178.2 0.8 copy.40
  179.0 0.6 copy.48
Async XLA Ops:
  0.6 15.0 %copy-start.7 = (f32[2048]{0:T(1024)S(1)}, f32[2048]{0:T(1024)}, u32[]{:S(2)}) copy-start(f32[2048]{0:T(1024)} %param.19) | copy-start | bytes 24580
  6.6 0.7 copy-start.6
  13.0 1.3 copy-start
  14.3 1.3 copy-start.4
  47.1 1.4 copy-start.2
  48.5 1.3 copy-start.5
  71.9 1.4 copy-start.3
  73.3 82.0 %copy-start.1 = (bf16[256,4096]{1,0:T(8,128)(2,1)S(1)}, bf16[256,4096]{1,0:T(8,128)(2,1)}, u32[]{:S(2)}) copy-start(bf16[256,4096]{1,0:T(8,128)(2,1)} %copy-done) | copy-start | bytes 6291460

commit v2 on v0

v2 whole, which is shorter than its diff:
```python
import functools
import math

import jax
import jax.numpy as jnp
from jax import lax
from jax.experimental import pallas as pl
from jax.experimental.pallas import tpu as pltpu
from jax.sharding import PartitionSpec as P

EPS = 1e-05
HIGH = lax.Precision.HIGHEST
F32 = jnp.float32
BF16 = jnp.bfloat16
MESH = pl.DeviceIdType.MESH
VMEM_LIMIT = 60 * 1024 * 1024
RING, CORES = 4, 2


def split(value):
    high = value.astype(BF16)
    return high, (value - high.astype(F32)).astype(BF16)


def dot(left, right):
    return jnp.dot(left, right, preferred_element_type=F32)


def dot_nt(left, right):
    return lax.dot_general(left, right, (((1,), (1,)), ((), ())), preferred_element_type=F32)


def softplus(value):
    return jnp.maximum(value, 0.0) + jnp.log1p(jnp.exp(-jnp.abs(value)))


def sigmoid(value):
    return 1.0 / (1.0 + jnp.exp(-value))


def lower(length):
    row = lax.broadcasted_iota(jnp.int32, (length, length), 0)
    column = lax.broadcasted_iota(jnp.int32, (length, length), 1)
    return row >= column


def loop(count, body):
    def one(at, carry):
        body(at)
        return carry

    lax.fori_loop(0, count, one, 0)


def wide(parts):
    return jnp.concatenate(parts, axis=1)


def tall(parts):
    return jnp.concatenate(parts, axis=0)


def mixer_kernel(
    scale,
    groups,
    limit_ref,
    x_hbm,
    gate_hbm,
    out_hbm,
    dt_ref,
    b_ref,
    c_ref,
    a_ref,
    bias_ref,
    skip_ref,
    gain_ref,
    gx_hbm,
    ggate_hbm,
    gdt_ref,
    gb_ref,
    gc_ref,
    small_out,
    gain_out,
    x_in,
    gate_in,
    out_in,
    xh,
    xs_high,
    xs_low,
    esb,
    erb,
    cots,
    silus,
    slopes,
    mixed,
    y_high,
    y_low,
    fresh,
    carried,
    local,
    behind,
    sib,
    pair,
    scat,
    pref,
    ret,
    total,
    ztotal,
    causal_m,
    causal_t,
    bt,
    bb,
    cc,
    ctct,
    ec_ref,
    decays,
    gains,
    skip_line,
    row_ref,
    rho_ref,
    sigma_ref,
    square,
    cross,
    grad_m,
    grad_c,
    grad_b,
    halves,
    ggain,
    gskip,
    rows,
    gain_swap,
    gain_all,
    small_swap,
    small_all,
    in_sem,
    out_sem,
    decay_send,
    decay_recv,
    send_sem,
    recv_sem,
    gain_send,
    gain_recv,
    small_send,
    small_recv,
):
    tokens, heads, dim = x_in.shape
    per = heads // groups
    half = per // CORES
    own = half // RING
    count = lax.axis_size("ctx")
    me = lax.axis_index("ctx")
    ring_len = RING * CORES
    z = me // ring_len
    q = lax.rem(me, ring_len)
    y = q // CORES
    c = lax.rem(q, CORES)
    mine = lax.axis_index("fsdp")
    other = 1 - mine

    def copy_in(at):
        source, target = ((x_hbm, x_in), (gate_hbm, gate_in), (out_hbm, out_in))[at]
        return pltpu.make_async_copy(source, target, in_sem.at[at])

    for at in range(3):
        copy_in(at).start()
    barrier = pltpu.get_barrier_semaphore()
    pl.semaphore_signal(barrier, inc=1, device_id={"fsdp": other}, device_id_type=MESH)
    for hop in range(1, count):
        pl.semaphore_signal(
            barrier, inc=1, device_id={"ctx": lax.rem(me + hop, count)}, device_id_type=MESH
        )

    diagonal = lax.broadcasted_iota(jnp.int32, (heads, heads), 0) == lax.broadcasted_iota(
        jnp.int32, (heads, heads), 1
    )

    def column(ref):
        return jnp.sum(jnp.where(diagonal, ref[...], 0.0), axis=1, keepdims=True)

    rate = -jnp.exp(column(a_ref))
    bias = column(bias_ref)
    skip_line[...] = jnp.broadcast_to(column(skip_ref), skip_line.shape)
    step = softplus(dt_ref[...].astype(F32) + bias)
    ones = jnp.where(lower(tokens), 1.0, 0.0).astype(F32)
    running = lax.dot_general(
        step * rate, ones, (((1,), (1,)), ((), ())), precision=HIGH, preferred_element_type=F32
    )
    middle = 0.5 * running[:, tokens - 1 :]
    er = jnp.transpose(jnp.exp(running - middle))
    es = jnp.transpose(jnp.exp(middle - running) * step)
    ec = jnp.exp(middle)
    ec_ref[...] = jnp.broadcast_to(ec, ec_ref.shape)
    decays[q] = jnp.broadcast_to(ec * ec, ec_ref.shape)

    pl.semaphore_wait(barrier, count)

    def decay_copy(hop):
        return pltpu.make_async_remote_copy(
            src_ref=decays.at[q],
            dst_ref=decays.at[q],
            send_sem=decay_send.at[hop],
            recv_sem=decay_recv.at[hop],
            device_id={"ctx": z * ring_len + lax.rem(q + hop, ring_len)},
            device_id_type=MESH,
        )

    for hop in range(1, ring_len):
        decay_copy(hop).start()

    def gain_copy():
        return pltpu.make_async_remote_copy(
            src_ref=gain_ref,
            dst_ref=gains.at[mine],
            send_sem=gain_send.at[0],
            recv_sem=gain_recv.at[0],
            device_id={"fsdp": other},
            device_id_type=MESH,
        )

    gain_copy().start()
    gains[mine] = gain_ref[...]

    halves[...] = b_ref[...].astype(F32)
    b_groups = [halves[pl.ds(g, tokens, stride=groups), :] for g in range(groups)]
    halves[...] = c_ref[...].astype(F32)
    c_groups = [halves[pl.ds(g, tokens, stride=groups), :] for g in range(groups)]
    for g in range(groups):
        b_one, c_one = b_groups[g].astype(BF16), c_groups[g].astype(BF16)
        b_turn = jnp.transpose(b_groups[g]).astype(BF16)
        c_turn = jnp.transpose(c_groups[g]).astype(BF16)
        bt[g] = wide([b_turn, b_turn])
        bb[g] = wide([b_one, b_one])
        cc[g] = wide([c_one, c_one])
        ctct[g] = wide([c_turn, c_turn])

    def remote(later, g, which, source, target, device):
        at = (int(later) * groups + g) * 9 + which
        return pltpu.make_async_remote_copy(
            src_ref=source,
            dst_ref=target,
            send_sem=send_sem.at[at],
            recv_sem=recv_sem.at[at],
            device_id={"ctx": device},
            device_id_type=MESH,
        )

    sibling = z * ring_len + y * CORES + (1 - c)

    def ring_device(hop):
        return z * ring_len + lax.rem(y + hop, RING) * CORES + c

    def first_swap(later, g):
        source = local if later else fresh
        return remote(
            later,
            g,
            0,
            source.at[pl.ds(g * per + (1 - c) * half, half)],
            sib.at[pl.ds(g * half, half)],
            sibling,
        )

    def scatter(later, g, hop):
        to = lax.rem(y + hop, RING)
        return remote(
            later,
            g,
            hop,
            pair.at[pl.ds(g * half + to * own, own)],
            scat.at[pl.ds(g * half + y * own, own)],
            ring_device(hop),
        )

    def cross_z(later, g):
        return remote(
            later,
            g,
            7,
            total.at[pl.ds(g * own, own)],
            ztotal.at[pl.ds(g * own, own)],
            (1 - z) * ring_len + q,
        )

    def give_back(later, g, hop):
        to = lax.rem(y + hop, RING)
        return remote(
            later,
            g,
            3 + hop,
            pref.at[pl.ds(g * half + to * own, own)],
            ret.at[pl.ds(g * half + y * own, own)],
            ring_device(hop),
        )

    def second_swap(later, g):
        target = behind if later else carried
        return remote(
            later,
            g,
            8,
            ret.at[pl.ds(g * half, half)],
            target.at[pl.ds(g * per + c * half, half)],
            sibling,
        )

    def combine(later, g):
        source = local if later else fresh
        second = 0 if later else 1
        first_swap(later, g).wait()

        def one(k):
            head = g * per + c * half + k
            decay = decays[y * CORES + second, pl.ds(head, 1), :]
            is_second = c == second
            mul_own = jnp.where(is_second, 1.0, decay)
            mul_sib = jnp.where(is_second, decay, 1.0)
            value = source[head] * mul_own + sib[g * half + k] * mul_sib
            pair[g * half + k] = value

        loop(half, one)
        for hop in range(1, RING):
            scatter(later, g, hop).start()
        for j in range(own):
            scat[g * half + y * own + j] = pair[g * half + y * own + j]

    def prefixes(later, g):
        for hop in range(1, RING):
            scatter(later, g, hop).wait()
        order = list(range(RING))[:: -1 if later else 1]
        for j in range(own):
            head = g * per + c * half + y * own + j
            state = jnp.zeros_like(scat[0])
            for chip in order:
                decay = decays[chip * CORES, pl.ds(head, 1), :] * decays[chip * CORES + 1, pl.ds(head, 1), :]
                pref[g * half + chip * own + j] = state
                state = scat[g * half + chip * own + j] + decay * state
            total[g * own + j] = state

        @pl.when(z == (1 if later else 0))
        def _():
            cross_z(later, g).start()
            for hop in range(1, RING):
                give_back(later, g, hop).start()

    def second_chips(later, g):
        @pl.when(z == (0 if later else 1))
        def _():
            cross_z(later, g).wait_recv()
            order = list(range(RING))[:: -1 if later else 1]
            for j in range(own):
                head = g * per + c * half + y * own + j
                state = ztotal[g * own + j]
                for chip in order:
                    decay = decays[chip * CORES, pl.ds(head, 1), :] * decays[chip * CORES + 1, pl.ds(head, 1), :]
                    pref[g * half + chip * own + j] += state
                    state = decay * state
            for hop in range(1, RING):
                give_back(later, g, hop).start()

    def returned(later, g):
        source = local if later else fresh
        target = behind if later else carried
        first = 1 if later else 0
        for j in range(own):
            ret[g * half + y * own + j] = pref[g * half + y * own + j]
        for hop in range(1, RING):
            give_back(later, g, hop).wait()

        @pl.when(z == (1 if later else 0))
        def _():
            cross_z(later, g).wait_send()

        def one(k):
            head = g * per + c * half + k
            decay = decays[y * CORES + first, pl.ds(head, 1), :]
            is_first = c == first
            before = ret[g * half + k]
            base = jnp.where(is_first, source[head], sib[g * half + k])
            after = base + decay * before
            target[head] = jnp.where(is_first, before, after)
            ret[g * half + k] = jnp.where(is_first, after, before)

        loop(half, one)
        second_swap(later, g).start()

    def states(g):
        temp = cots.at[g]
        temp[...] = x_in[:, g * per : (g + 1) * per, :].astype(F32).reshape(tokens * per, dim)
        for one in range(per):
            esb[g * per + one] = jnp.broadcast_to(
                es[:, g * per + one : g * per + one + 1], (tokens, dim)
            )

        def pair_at(hh):
            scaled = []
            for at in range(2):
                head = g * per + hh + at
                x_one = temp[pl.ds(hh + at, tokens, stride=per), :]
                xh[head] = x_one.astype(BF16)
                high, low = split(x_one * esb[head])
                xs_high[head] = high
                xs_low[head] = low
                scaled.append(tall([high, low]))
            state = dot(bt[g], wide(scaled))
            for at in range(2):
                head = g * per + hh + at
                fresh[head] = state[:, at * dim : (at + 1) * dim] * ec_ref[pl.ds(head, 1), :]

        loop(half // 2, lambda i: pair_at((1 - c) * half + 2 * i))
        first_swap(False, g).start()
        loop(half // 2, lambda i: pair_at(c * half + 2 * i))

    def scores(g):
        value = jnp.where(lower(tokens), dot(cc[g, :, :dim], bt[g, :, :tokens]), 0.0)
        high, low = split(value)
        causal_m[g] = wide([high, high, low])
        high, low = split(jnp.transpose(value))
        causal_t[g] = wide([high, high, low])

    def widen(g):
        temp = cots.at[g]
        temp[...] = gate_in[:, g * per : (g + 1) * per, :].astype(F32).reshape(tokens * per, dim)

        def one(hh):
            gate = temp[pl.ds(hh, tokens, stride=per), :]
            sig = sigmoid(gate)
            silu = gate * sig
            place = pl.ds(pl.multiple_of(hh * tokens, tokens), tokens)
            silus[g, place, :] = silu
            slopes[g, place, :] = sig + silu * (1.0 - sig)

        loop(per, one)
        keep = lax.broadcasted_iota(jnp.int32, (tokens, 1, 1), 0) < limit_ref[0]
        temp[...] = jnp.where(
            keep, out_in[:, g * per : (g + 1) * per, :].astype(F32), 0.0
        ).reshape(tokens * per, dim)

    def inside(g):
        for one in range(per):
            erb[g * per + one] = jnp.broadcast_to(
                er[:, g * per + one : g * per + one + 1], (tokens, dim)
            )

        def pair_at(i):
            hh = g * per + 2 * i
            right = wide(
                [tall([xs_high[hh + at], xs_low[hh + at], xs_high[hh + at]]) for at in range(2)]
            )
            scanned = dot(causal_m[g], right)
            for at in range(2):
                head = hh + at
                mixed[head] = scanned[:, at * dim : (at + 1) * dim] * erb[head] + xh[head].astype(
                    F32
                ) * skip_line[pl.ds(head, 1), :]

        loop(per // 2, pair_at)

    def gated_norm(g):
        square[...] = jnp.zeros_like(square)
        cross[...] = jnp.zeros_like(cross)

        def pair_at(i):
            hh = 2 * i
            right = []
            for at in range(2):
                head = g * per + hh + at
                right.append(tall(split(carried[head] * ec_ref[pl.ds(head, 1), :])))
            scanned = dot(cc[g], wide(right))
            sum_square, sum_cross = square[...], cross[...]
            for at in range(2):
                head = g * per + hh + at
                mix = mixed[head] + scanned[:, at * dim : (at + 1) * dim] * erb[head]
                mixed[head] = mix
                place = pl.ds(pl.multiple_of((hh + at) * tokens, tokens), tokens)
                gated = mix * silus[g, place, :]
                cot = cots[g, pl.ds(hh + at, tokens, stride=per), :]
                upper = cot * gains[g, pl.ds(hh + at, 1), :]
                sum_square = sum_square + gated * gated
                sum_cross = sum_cross + upper * gated
            square[...] = sum_square
            cross[...] = sum_cross

        loop(per // 2, pair_at)
        width = per * dim
        inverse = lax.rsqrt(jnp.sum(square[...], axis=1, keepdims=True) * (1.0 / width) + EPS)
        pull = inverse * inverse * inverse * (jnp.sum(cross[...], axis=1, keepdims=True) * (1.0 / width))
        square[...] = jnp.broadcast_to(inverse, square.shape)
        cross[...] = jnp.broadcast_to(pull, cross.shape)

    lane = lax.broadcasted_iota(jnp.int32, (tokens, per), 1)

    def put(ref, g, hh, value):
        ref[g] = jnp.where(lane == hh, value, ref[g])

    def pulled(g):
        rho_ref[g] = jnp.zeros((tokens, per), F32)

        def pair_at(hh):
            right = []
            for at in range(2):
                head = g * per + hh + at
                row = pl.ds(head, 1)
                place = pl.ds(pl.multiple_of((hh + at) * tokens, tokens), tokens)
                silu = silus[g, place, :]
                mix = mixed[head]
                gated = mix * silu
                natural = pl.ds(hh + at, tokens, stride=per)
                cot = cots[g, natural, :]
                inverse = square[...]
                ggain[row, :] = jnp.sum(cot * gated * inverse, axis=0, keepdims=True)
                grad_gated = inverse * (cot * gains[g, pl.ds(hh + at, 1), :]) - cross[...] * gated
                grad_mix = grad_gated * silu
                cots[g, natural, :] = grad_gated * mix * slopes[g, place, :]
                x_one = xh[head].astype(F32)
                skip = skip_line[row, :]
                gskip[row, :] = jnp.sum(grad_mix * x_one, axis=0, keepdims=True)
                put(
                    rho_ref,
                    g,
                    hh + at,
                    jnp.sum(grad_mix * (mix - x_one * skip), axis=1, keepdims=True),
                )
                mixed[head] = grad_mix * skip
                high, low = split(grad_mix * erb[head])
                y_high[head] = high
                y_low[head] = low
                right.append(tall([high, low]))
            back = dot(ctct[g], wide(right))
            for at in range(2):
                head = g * per + hh + at
                local[head] = back[:, at * dim : (at + 1) * dim] * ec_ref[pl.ds(head, 1), :]

        loop(half // 2, lambda i: pair_at((1 - c) * half + 2 * i))
        first_swap(True, g).start()
        loop(half // 2, lambda i: pair_at(c * half + 2 * i))

    def gate_copy(g):
        place = pl.ds(g * per, per)
        return pltpu.make_async_copy(
            gate_in.at[:, place, :], ggate_hbm.at[:, place, :], out_sem.at[g]
        )

    def x_copy(g):
        place = pl.ds(g * per, per)
        return pltpu.make_async_copy(
            x_in.at[:, place, :], gx_hbm.at[:, place, :], out_sem.at[groups + g]
        )

    def inner_part(g, hh, grad_scaled):
        for at in range(2):
            head = g * per + hh + at
            inner = grad_scaled[:, at * dim : (at + 1) * dim] * esb[head]
            put(
                sigma_ref,
                g,
                hh + at,
                jnp.sum(inner * xh[head].astype(F32), axis=1, keepdims=True),
            )
            yield at, head, inner

    def inside_back(g):
        gate_in[:, g * per : (g + 1) * per, :] = cots[g].reshape(tokens, per, dim).astype(BF16)
        gate_copy(g).start()
        grad_m[...] = jnp.zeros_like(grad_m)
        grad_c[...] = jnp.zeros_like(grad_c)

        def pair_at(i):
            hh = 2 * i
            head = g * per + hh
            yh = wide([y_high[head], y_high[head + 1]])
            yl = wide([y_low[head], y_low[head + 1]])
            x_high = wide([xs_high[head], xs_high[head + 1]])
            x_low = wide([xs_low[head], xs_low[head + 1]])
            left = wide([yh, yh, yl])
            grad_m[...] += dot_nt(left, wide([x_high, x_low, x_high]))
            s_high, s_low = split(
                wide(
                    [carried[head + at] * ec_ref[pl.ds(head + at, 1), :] for at in range(2)]
                )
            )
            grad_c[...] += dot_nt(left, wide([s_high, s_low, s_high]))
            grad_scaled = dot(causal_t[g], tall([yh, yl, yh]))
            for at in range(2):
                one = head + at
                inner = grad_scaled[:, at * dim : (at + 1) * dim] * esb[one]
                put(
                    sigma_ref,
                    g,
                    hh + at,
                    jnp.sum(inner * xh[one].astype(F32), axis=1, keepdims=True),
                )
                mixed[one] += inner
                decay = ec_ref[pl.ds(one, 1), :]
                fresh[one] += (decay * decay) * carried[one]

        sigma_ref[g] = jnp.zeros((tokens, per), F32)
        loop(per // 2, pair_at)
        value = jnp.where(lower(tokens), grad_m[...], 0.0)
        high, low = split(value)
        part = grad_c[...] + dot(wide([high, low]), tall([bb[g, :, :dim], bb[g, :, :dim]]))
        halves[pl.ds(g, tokens, stride=groups), :] = part
        high, low = split(jnp.transpose(value))
        grad_b[g] = dot(wide([high, low]), tall([cc[g, :, :dim], cc[g, :, :dim]]))

    def last(g):
        wide_x = silus.at[g]

        def pair_at(i):
            hh = 2 * i
            head = g * per + hh
            parts = []
            for at in range(2):
                one = head + at
                decay = ec_ref[pl.ds(one, 1), :]
                rows[pl.ds(one, 1), :] = jnp.sum(behind[one] * fresh[one], axis=0, keepdims=True)
                parts.append(behind[one] * decay)
            s_high, s_low = split(wide(parts))
            x_high = wide([xs_high[head], xs_high[head + 1]])
            x_low = wide([xs_low[head], xs_low[head + 1]])
            grad_b[g] += dot_nt(wide([x_high, x_high, x_low]), wide([s_high, s_low, s_high]))
            grad_scaled = dot(bb[g], tall([s_high, s_low]))
            for at in range(2):
                one = head + at
                inner = grad_scaled[:, at * dim : (at + 1) * dim] * esb[one]
                more = jnp.sum(inner * xh[one].astype(F32), axis=1, keepdims=True)
                sigma_ref[g] += jnp.where(lane == hh + at, more, 0.0)
                wide_x[pl.ds(hh + at, tokens, stride=per), :] = mixed[one] + inner

        loop(per // 2, pair_at)
        x_in[:, g * per : (g + 1) * per, :] = wide_x[...].reshape(tokens, per, dim).astype(BF16)
        x_copy(g).start()
        here = slice(g * per, (g + 1) * per)
        sums = lax.dot_general(
            rho_ref[g] - sigma_ref[g],
            jnp.where(lower(tokens), 1.0, 0.0).astype(F32),
            (((0,), (0,)), ((), ())),
            precision=HIGH,
            preferred_element_type=F32,
        )
        grad_log = sums + jnp.sum(rows[here, :], axis=1, keepdims=True)
        bias_here = column(bias_ref)[here]
        rate_here = -jnp.exp(column(a_ref)[here])
        value = dt_ref[here, :].astype(F32) + bias_here
        step_here = softplus(value)
        grad_dt = (jnp.transpose(sigma_ref[g]) / step_here + grad_log * rate_here) * sigmoid(value)
        gdt_ref[here, :] = grad_dt.astype(BF16)
        return (
            jnp.sum(grad_log * step_here, axis=1, keepdims=True) * rate_here,
            jnp.sum(grad_dt, axis=1, keepdims=True),
            jnp.sum(gskip[here, :], axis=1, keepdims=True),
        )

    def swap_copy(source, target, sems):
        return pltpu.make_async_remote_copy(
            src_ref=source,
            dst_ref=target,
            send_sem=sems[0].at[1],
            recv_sem=sems[1].at[1],
            device_id={"fsdp": other},
            device_id_type=MESH,
        )

    def all_copy(ref, sems, hop):
        return pltpu.make_async_remote_copy(
            src_ref=ref.at[0],
            dst_ref=ref.at[hop],
            send_sem=sems[0].at[1 + hop],
            recv_sem=sems[1].at[1 + hop],
            device_id={"ctx": lax.rem(me + hop, count)},
            device_id_type=MESH,
        )

    gain_sems, small_sems = (gain_send, gain_recv), (small_send, small_recv)

    def gain_swap_copy():
        return swap_copy(
            ggain.at[pl.ds(pl.multiple_of(other * per, per), per)], gain_swap, gain_sems
        )

    copy_in(0).wait()
    states(0)
    for hop in range(1, ring_len):
        decay_copy(hop).wait()
    combine(False, 0)
    states(1)
    combine(False, 1)
    scores(0)
    scores(1)
    inside(0)
    copy_in(1).wait()
    copy_in(2).wait()
    prefixes(False, 0)
    widen(0)
    second_chips(False, 0)
    inside(1)
    prefixes(False, 1)
    widen(1)
    second_chips(False, 1)
    gain_copy().wait()
    returned(False, 0)
    second_swap(False, 0).wait()
    gated_norm(0)
    pulled(0)
    returned(False, 1)
    combine(True, 0)
    second_swap(False, 1).wait()
    gated_norm(1)
    prefixes(True, 0)
    pulled(1)
    second_chips(True, 0)
    combine(True, 1)
    gain_swap_copy().start()
    inside_back(0)
    returned(True, 0)
    prefixes(True, 1)
    gain_swap_copy().wait()
    gain_all[0] = gain_swap[...] + ggain[pl.ds(pl.multiple_of(mine * per, per), per), :]
    for hop in range(1, count):
        all_copy(gain_all, gain_sems, hop).start()
    inside_back(1)
    gc_ref[...] = halves[...].astype(BF16)
    second_chips(True, 1)
    second_swap(True, 0).wait()
    sums = [last(0)]
    returned(True, 1)
    second_swap(True, 1).wait()
    sums.append(last(1))
    turn = lax.broadcasted_iota(jnp.int32, (per, dim), 0) == lax.broadcasted_iota(
        jnp.int32, (per, dim), 1
    )
    shifted = lax.broadcasted_iota(jnp.int32, (per, dim), 0) + per == lax.broadcasted_iota(
        jnp.int32, (per, dim), 1
    )
    small_all[0] = jnp.zeros(small_out.shape, F32)
    for at in range(3):
        small_all[0, at : at + 1, :] = jnp.sum(
            jnp.where(turn, sums[0][at], 0.0) + jnp.where(shifted, sums[1][at], 0.0),
            axis=0,
            keepdims=True,
        )
    small_mine = swap_copy(small_all.at[0], small_swap, small_sems)
    small_mine.start()
    for g in range(groups):
        halves[pl.ds(g, tokens, stride=groups), :] = grad_b[g]
    gb_ref[...] = halves[...].astype(BF16)
    for hop in range(1, count):
        all_copy(gain_all, gain_sems, hop).wait()
    gain_total = gain_all[0]
    for hop in range(1, count):
        gain_total = gain_total + gain_all[hop]
    gain_out[...] = gain_total * scale
    small_mine.wait()
    small_all[0] += small_swap[...]
    for hop in range(1, count):
        all_copy(small_all, small_sems, hop).start()
    for hop in range(1, count):
        all_copy(small_all, small_sems, hop).wait()
    small_total = small_all[0]
    for hop in range(1, count):
        small_total = small_total + small_all[hop]
    small_out[...] = small_total * scale
    for g in range(groups):
        gate_copy(g).wait()
        x_copy(g).wait()


def per_device(
    x_input,
    gate_input,
    dt_raw,
    b_input,
    c_input,
    a_log,
    dt_bias,
    skip_weight,
    norm_gain,
    valid_len,
    grad_output,
):
    _, tokens, heads, dim = x_input.shape
    groups, state = b_input.shape[2:]
    per = heads // groups
    half = per // CORES
    own = half // RING
    count = lax.axis_size("ctx")
    ring_len = RING * CORES
    shape = jax.ShapeDtypeStruct
    whole = pl.BlockSpec(memory_space=pltpu.VMEM)
    anywhere = pl.BlockSpec(memory_space=pl.ANY)
    limit = valid_len - lax.axis_index("ctx") * tokens
    scale = 1.0 / math.sqrt(tokens * count * lax.axis_size("fsdp"))
    sems = pltpu.SemaphoreType.DMA

    def vmem(*dims, kind=F32):
        return pltpu.VMEM(dims, kind)

    scratch = [
        vmem(tokens, heads, dim, kind=BF16),
        vmem(tokens, heads, dim, kind=BF16),
        vmem(tokens, heads, dim, kind=BF16),
        vmem(heads, tokens, dim, kind=BF16),
        vmem(heads, tokens, dim, kind=BF16),
        vmem(heads, tokens, dim, kind=BF16),
        vmem(heads, tokens, dim),
        vmem(heads, tokens, dim),
        vmem(groups, tokens * per, dim),
        vmem(groups, tokens * per, dim),
        vmem(groups, tokens * per, dim),
        vmem(heads, tokens, dim),
        vmem(heads, tokens, dim, kind=BF16),
        vmem(heads, tokens, dim, kind=BF16),
        vmem(heads, state, dim),
        vmem(heads, state, dim),
        vmem(heads, state, dim),
        vmem(heads, state, dim),
        vmem(groups * half, state, dim),
        vmem(groups * half, state, dim),
        vmem(groups * half, state, dim),
        vmem(groups * half, state, dim),
        vmem(groups * half, state, dim),
        vmem(groups * own, state, dim),
        vmem(groups * own, state, dim),
        vmem(groups, tokens, 3 * tokens, kind=BF16),
        vmem(groups, tokens, 3 * tokens, kind=BF16),
        vmem(groups, state, 2 * tokens, kind=BF16),
        vmem(groups, tokens, 2 * state, kind=BF16),
        vmem(groups, tokens, 2 * state, kind=BF16),
        vmem(groups, state, 2 * tokens, kind=BF16),
        vmem(heads, dim),
        vmem(ring_len, heads, dim),
        vmem(groups, per, dim),
        vmem(heads, dim),
        vmem(8, dim),
        vmem(groups, tokens, per),
        vmem(groups, tokens, per),
        vmem(tokens, dim),
        vmem(tokens, dim),
        vmem(tokens, tokens),
        vmem(tokens, state),
        vmem(groups, tokens, state),
        vmem(tokens * groups, state),
        vmem(heads, dim),
        vmem(heads, dim),
        vmem(heads, dim),
        vmem(per, dim),
        vmem(count, per, dim),
        vmem(8, dim),
        vmem(count, 8, dim),
        sems((3,)),
        sems((2 * groups,)),
        sems((ring_len,)),
        sems((ring_len,)),
        sems((2 * groups * 9,)),
        sems((2 * groups * 9,)),
        sems((1 + count,)),
        sems((1 + count,)),
        sems((1 + count,)),
        sems((1 + count,)),
    ]
    grad_x, ggate, grad_dt, grad_b, grad_c, small, gain = pl.pallas_call(
        functools.partial(mixer_kernel, scale, groups),
        in_specs=[pl.BlockSpec(memory_space=pltpu.SMEM), anywhere, anywhere, anywhere] + [whole] * 7,
        out_specs=[anywhere, anywhere] + [whole] * 5,
        out_shape=[
            shape((tokens, heads, dim), BF16),
            shape((tokens, heads, dim), BF16),
            shape((heads, tokens), BF16),
            shape((tokens * groups, state), BF16),
            shape((tokens * groups, state), BF16),
            shape((8, dim), F32),
            shape((per, dim), F32),
        ],
        scratch_shapes=scratch,
        compiler_params=pltpu.CompilerParams(
            collective_id=0, has_side_effects=True, vmem_limit_bytes=VMEM_LIMIT
        ),
        name="mixer",
    )(
        limit,
        x_input[0],
        gate_input[0],
        grad_output[0],
        dt_raw[0],
        b_input.reshape(tokens * groups, state),
        c_input.reshape(tokens * groups, state),
        a_log.reshape(1, heads),
        dt_bias.reshape(1, heads),
        skip_weight.reshape(1, heads),
        norm_gain.reshape(per, dim),
    )
    return (
        grad_x[None],
        ggate[None],
        grad_dt[None],
        grad_b.reshape(b_input.shape),
        grad_c.reshape(c_input.shape),
        small[0, :heads],
        small[1, :heads],
        small[2, :heads],
        gain.reshape(norm_gain.shape),
    )


def solution(mesh):
    placed = (
        P("fsdp", "ctx", "tp", None),
        P("fsdp", "ctx", "tp", None),
        P("fsdp", "tp", "ctx"),
        P("fsdp", "ctx", "tp", None),
        P("fsdp", "ctx", "tp", None),
        P("tp"),
        P("tp"),
        P("tp"),
        P(("tp", "fsdp")),
        P("fsdp"),
        P("fsdp", "ctx", "tp", None),
    )
    return jax.shard_map(
        per_device,
        mesh=mesh,
        in_specs=placed,
        out_specs=(
            P("fsdp", "ctx", "tp", None),
            P("fsdp", "ctx", "tp", None),
            P("fsdp", "tp", "ctx"),
            P("fsdp", "ctx", "tp", None),
            P("fsdp", "ctx", "tp", None),
            P("tp"),
            P("tp"),
            P("tp"),
            P(("tp", "fsdp")),
        ),
        check_vma=False,
    )
```

time: 652 us -> 105 us (0.16); the launches traced: 644 us -> 105 us
  waiting for transfers between devices: 213 us -> 0 us
  blocking collectives: 171 us -> 0 us
  other arithmetic: 104 us -> 0 us
  Pallas kernels: 0 us -> 95 us
  matrix products: 77.9 us -> 0 us
  local copies, waits for them, and re-layouts: 61.6 us -> 8.58 us
  between operations: 16.3 us -> 1.32 us
    all_gather x2 -> x0, waiting for transfers between devices: 213 us -> none  [prefix(): gathered = jax.tree.map(lambda a: lax.all_gather(a, axis), part)]
    psum x2 -> x0, blocking collectives: 134 us -> none  [the longest x1 68.8 us: per_device(): head_totals = lax.psum((grad_a, grad_bias, grad_skip), ('ctx', 'fsdp'))]
    pallas_call x0 -> x1, Pallas kernels: none -> 95 us  [per_device(): pl.pallas_call(functools.partial(mixer_kernel, scale, groups), in_specs=[...]
    dot_general x14 -> x0, matrix products: 77.9 us -> none  [the longest x3 37.2 us: block_step(): output = jnp.einsum('gkts,sgkp->tgkp', weights, x_block, precision=HIGH)]
    add x17 -> x0, other arithmetic: 56.5 us -> none  [the longest x15 55.8 us: join_states(): later[1] + jnp.exp(later[0])[..., None, None] * earlier[1]]
    all_gather x2 -> x0, blocking collectives: 26.8 us -> none  [the longest x1 21.7 us: prefix(): gathered = jax.tree.map(lambda a: lax.all_gather(a, axis), part)]
    reduce_sum x7 -> x0, other arithmetic: 24.4 us -> none  [the longest x1 10.1 us: mixer_forward(): mixed = scanned + skip_weight[None, :, :, None] * x_all]
    another operation x12 -> x0, other arithmetic: 12.9 us -> none
  transfers between devices with their start and end apart: 2 -> 0, of which waited for: 2 -> 0; matrix products, arithmetic and copies ran while one was open for 10% -> 0% of each run, Pallas kernels for 0% -> 0%
where the time goes in v2:
time: 105 us
  Pallas kernels  95 us (90%)
  local copies, waits for them, and re-layouts  8.58 us (8%)
  between operations  1.32 us (1%)
    pallas_call x1, Pallas kernels, per_device(): pl.pallas_call(functools.partial(mixer_kernel, scale, groups), in_specs=[...  95 us
    unnamed x16, local copies, waits for them, and re-layouts  7.27 us

profile of v2, /device:TPU:1, one launch (start us, length us, event | category | flops | bytes accessed | tf_op | source)
XLA Modules:
  0.0 104.9 jit_solution(13693153622365592218)
XLA Ops:
  1.3 95.0 %mixer.1 = (bf16[256,32,128]{2,1,0:T(8,128)(2,1)}, bf16[256,32,128]{2,1,0:T(8,128)(2,1)}, bf16[32,256]{1,0:T(8,128)(2,1)}, bf16[512,128]{1,0:T(8,128)(2,1)}, bf1...) custom-call(s32[1]{0:T(128)S(6)} %sub.7.limit_ref, bf16[256,32,128]{2,1,0:T(8,128)(2,1)} %bitcast.23, ...), custom_call_target="tpu_custom_call" | custom-call | tf_op jit(solution)/shard_map/mixer/pallas_call | solution.py:860
  96.3 1.3 %slice_bitcast_fusion = (f32[32]{0:T(128)}, f32[32]{0:T(128)}, f32[32]{0:T(128)}) fusion(f32[8,128]{1,0:T(8,128)} %get-tuple-element.21), kind=kLoop, calls=%fused_computation | loop fusion | bytes 768 | tf_op jit(solution)/shard_map/squeeze | solution.py:899
  97.6 0.0 copy-start
  97.6 3.4 %copy.27 = bf16[1,256,32,128]{3,2,1,0:T(8,128)(2,1)} copy(bf16[1,256,32,128]{3,2,1,0:T(8,128)(2,1)} %bitcast.27) | data formatting | bytes 4194304
  101.0 0.0 copy-done
  101.0 0.0 copy-start.3
  101.0 0.0 copy-start.2
  101.0 0.0 copy-start.1
  101.0 0.0 copy-start.4
  101.0 1.3 %copy.28 = bf16[1,256,32,128]{3,2,1,0:T(8,128)(2,1)} copy(bf16[1,256,32,128]{3,2,1,0:T(8,128)(2,1)S(1)} %bitcast.26) | data formatting | bytes 4194304
  102.3 0.0 copy-done.3
  102.3 0.6 copy.29
  102.9 0.0 copy-done.2
  102.9 0.7 copy.30
  103.6 0.0 copy-done.1
  103.6 0.7 copy.31
  104.3 0.0 copy-done.4
  104.3 0.6 copy.32
Async XLA Ops:
  97.6 3.4 %copy-start = (bf16[256,32,128]{2,1,0:T(8,128)(2,1)S(1)}, bf16[256,32,128]{2,1,0:T(8,128)(2,1)}, u32[]{:S(2)}) copy-start(bf16[256,32,128]{2,1,0:T(8,128)(2,1)} %get-tuple-element.17) | copy-start | bytes 6291460
  101.0 1.3 %copy-start.3 = (bf16[32,256]{1,0:T(8,128)(2,1)S(1)}, bf16[32,256]{1,0:T(8,128)(2,1)}, u32[]{:S(2)}) copy-start(bf16[32,256]{1,0:T(8,128)(2,1)} %get-tuple-element.18) | copy-start | bytes 49156
  101.0 1.9 %copy-start.2 = (bf16[512,128]{1,0:T(8,128)(2,1)S(1)}, bf16[512,128]{1,0:T(8,128)(2,1)}, u32[]{:S(2)}) copy-start(bf16[512,128]{1,0:T(8,128)(2,1)} %get-tuple-element.19) | copy-start | bytes 393220
  101.0 2.6 %copy-start.1 = (bf16[512,128]{1,0:T(8,128)(2,1)S(1)}, bf16[512,128]{1,0:T(8,128)(2,1)}, u32[]{:S(2)}) copy-start(bf16[512,128]{1,0:T(8,128)(2,1)} %get-tuple-element.20) | copy-start | bytes 393220
  101.0 3.3 %copy-start.4 = (f32[16,128]{1,0:T(8,128)S(1)}, f32[16,128]{1,0:T(8,128)}, u32[]{:S(2)}) copy-start(f32[16,128]{1,0:T(8,128)} %get-tuple-element.22) | copy-start | bytes 24580

commit v3 on v2

--- a/solution.py
+++ b/solution.py
@@ -9,7 +9,6 @@
 from jax.sharding import PartitionSpec as P
 
 EPS = 1e-05
-HIGH = lax.Precision.HIGHEST
 F32 = jnp.float32
 BF16 = jnp.bfloat16
 MESH = pl.DeviceIdType.MESH
@@ -24,6 +23,12 @@
 
 def dot(left, right):
     return jnp.dot(left, right, preferred_element_type=F32)
+
+
+def dot_ones(value, ones):
+    high, low = split(value)
+    lowest = (value - high.astype(F32) - low.astype(F32)).astype(BF16)
+    return dot(high, ones) + dot(low, ones) + dot(lowest, ones)
 
 
 def dot_nt(left, right):
@@ -116,7 +121,7 @@
     decays,
     gains,
     skip_line,
-    row_ref,
+    decay_rows,
     rho_ref,
     sigma_ref,
     square,
@@ -157,14 +162,24 @@
     mine = lax.axis_index("fsdp")
     other = 1 - mine
 
-    def copy_in(at):
+    def copy_in(at, g):
         source, target = ((x_hbm, x_in), (gate_hbm, gate_in), (out_hbm, out_in))[at]
-        return pltpu.make_async_copy(source, target, in_sem.at[at])
+        place = pl.ds(g * per, per)
+        return pltpu.make_async_copy(
+            source.at[:, place, :], target.at[:, place, :], in_sem.at[at * groups + g]
+        )
 
     for at in range(3):
-        copy_in(at).start()
+        for g in range(groups):
+            copy_in(at, g).start()
     barrier = pltpu.get_barrier_semaphore()
-    pl.semaphore_signal(barrier, inc=1, device_id={"fsdp": other}, device_id_type=MESH)
+    far = [
+        {"fsdp": other},
+        {"ctx": (1 - z) * ring_len + q},
+        {"ctx": (1 - z) * ring_len + q, "fsdp": other},
+    ]
+    for peer in (far[0], far[2]):
+        pl.semaphore_signal(barrier, inc=1, device_id=peer, device_id_type=MESH)
     for hop in range(1, count):
         pl.semaphore_signal(
             barrier, inc=1, device_id={"ctx": lax.rem(me + hop, count)}, device_id_type=MESH
@@ -181,31 +196,29 @@
     bias = column(bias_ref)
     skip_line[...] = jnp.broadcast_to(column(skip_ref), skip_line.shape)
     step = softplus(dt_ref[...].astype(F32) + bias)
-    ones = jnp.where(lower(tokens), 1.0, 0.0).astype(F32)
-    running = lax.dot_general(
-        step * rate, ones, (((1,), (1,)), ((), ())), precision=HIGH, preferred_element_type=F32
-    )
+    row = lax.broadcasted_iota(jnp.int32, (tokens, tokens), 0)
+    upto = row <= lax.broadcasted_iota(jnp.int32, (tokens, tokens), 1)
+    running = dot_ones(step * rate, jnp.where(upto, 1.0, 0.0).astype(BF16))
     middle = 0.5 * running[:, tokens - 1 :]
     er = jnp.transpose(jnp.exp(running - middle))
     es = jnp.transpose(jnp.exp(middle - running) * step)
     ec = jnp.exp(middle)
     ec_ref[...] = jnp.broadcast_to(ec, ec_ref.shape)
-    decays[q] = jnp.broadcast_to(ec * ec, ec_ref.shape)
-
-    pl.semaphore_wait(barrier, count)
+    own_lane = lax.broadcasted_iota(jnp.int32, (heads, dim), 0) == lax.broadcasted_iota(
+        jnp.int32, (heads, dim), 1
+    )
+    decay_row = jnp.sum(jnp.where(own_lane, ec * ec, 0.0), axis=0, keepdims=True)
+    decay_rows[q] = jnp.broadcast_to(decay_row, decay_rows.shape[1:])
 
     def decay_copy(hop):
         return pltpu.make_async_remote_copy(
-            src_ref=decays.at[q],
-            dst_ref=decays.at[q],
+            src_ref=decay_rows.at[q],
+            dst_ref=decay_rows.at[q],
             send_sem=decay_send.at[hop],
             recv_sem=decay_recv.at[hop],
             device_id={"ctx": z * ring_len + lax.rem(q + hop, ring_len)},
             device_id_type=MESH,
         )
-
-    for hop in range(1, ring_len):
-        decay_copy(hop).start()
 
     def gain_copy():
         return pltpu.make_async_remote_copy(
@@ -217,7 +230,6 @@
             device_id_type=MESH,
         )
 
-    gain_copy().start()
     gains[mine] = gain_ref[...]
 
     halves[...] = b_ref[...].astype(F32)
@@ -407,7 +419,13 @@
                 fresh[head] = state[:, at * dim : (at + 1) * dim] * ec_ref[pl.ds(head, 1), :]
 
         loop(half // 2, lambda i: pair_at((1 - c) * half + 2 * i))
+        if g == 0:
+            pl.semaphore_wait(barrier, count + 1)
         first_swap(False, g).start()
+        if g == 0:
+            for hop in range(1, ring_len):
+                decay_copy(hop).start()
+            gain_copy().start()
         loop(half // 2, lambda i: pair_at(c * half + 2 * i))
 
     def scores(g):
@@ -459,8 +477,7 @@
         square[...] = jnp.zeros_like(square)
         cross[...] = jnp.zeros_like(cross)
 
-        def pair_at(i):
-            hh = 2 * i
+        def pair_at(hh):
             right = []
             for at in range(2):
                 head = g * per + hh + at
@@ -480,7 +497,9 @@
             square[...] = sum_square
             cross[...] = sum_cross
 
-        loop(per // 2, pair_at)
+        loop(half // 2, lambda i: pair_at(c * half + 2 * i))
+        second_swap(False, g).wait()
+        loop(half // 2, lambda i: pair_at((1 - c) * half + 2 * i))
         width = per * dim
         inverse = lax.rsqrt(jnp.sum(square[...], axis=1, keepdims=True) * (1.0 / width) + EPS)
         pull = inverse * inverse * inverse * (jnp.sum(cross[...], axis=1, keepdims=True) * (1.0 / width))
@@ -546,26 +565,18 @@
             x_in.at[:, place, :], gx_hbm.at[:, place, :], out_sem.at[groups + g]
         )
 
-    def inner_part(g, hh, grad_scaled):
-        for at in range(2):
-            head = g * per + hh + at
-            inner = grad_scaled[:, at * dim : (at + 1) * dim] * esb[head]
-            put(
-                sigma_ref,
-                g,
-                hh + at,
-                jnp.sum(inner * xh[head].astype(F32), axis=1, keepdims=True),
+    def inside_back(g, part):
+        if part == 0:
+            gate_in[:, g * per : (g + 1) * per, :] = (
+                cots[g].reshape(tokens, per, dim).astype(BF16)
             )
-            yield at, head, inner
-
-    def inside_back(g):
-        gate_in[:, g * per : (g + 1) * per, :] = cots[g].reshape(tokens, per, dim).astype(BF16)
-        gate_copy(g).start()
-        grad_m[...] = jnp.zeros_like(grad_m)
-        grad_c[...] = jnp.zeros_like(grad_c)
+            gate_copy(g).start()
+            grad_m[...] = jnp.zeros_like(grad_m)
+            grad_c[...] = jnp.zeros_like(grad_c)
+            sigma_ref[g] = jnp.zeros((tokens, per), F32)
 
         def pair_at(i):
-            hh = 2 * i
+            hh = part * half + 2 * i
             head = g * per + hh
             yh = wide([y_high[head], y_high[head + 1]])
             yl = wide([y_low[head], y_low[head + 1]])
@@ -593,8 +604,9 @@
                 decay = ec_ref[pl.ds(one, 1), :]
                 fresh[one] += (decay * decay) * carried[one]
 
-        sigma_ref[g] = jnp.zeros((tokens, per), F32)
-        loop(per // 2, pair_at)
+        loop(half // 2, pair_at)
+        if part == 0:
+            return
         value = jnp.where(lower(tokens), grad_m[...], 0.0)
         high, low = split(value)
         part = grad_c[...] + dot(wide([high, low]), tall([bb[g, :, :dim], bb[g, :, :dim]]))
@@ -602,11 +614,8 @@
         high, low = split(jnp.transpose(value))
         grad_b[g] = dot(wide([high, low]), tall([cc[g, :, :dim], cc[g, :, :dim]]))
 
-    def last(g):
-        wide_x = silus.at[g]
-
-        def pair_at(i):
-            hh = 2 * i
+    def last_sums(g):
+        def pair_at(hh):
             head = g * per + hh
             parts = []
             for at in range(2):
@@ -614,35 +623,28 @@
                 decay = ec_ref[pl.ds(one, 1), :]
                 rows[pl.ds(one, 1), :] = jnp.sum(behind[one] * fresh[one], axis=0, keepdims=True)
                 parts.append(behind[one] * decay)
-            s_high, s_low = split(wide(parts))
-            x_high = wide([xs_high[head], xs_high[head + 1]])
-            x_low = wide([xs_low[head], xs_low[head + 1]])
-            grad_b[g] += dot_nt(wide([x_high, x_high, x_low]), wide([s_high, s_low, s_high]))
-            grad_scaled = dot(bb[g], tall([s_high, s_low]))
+            grad_scaled = dot(bb[g], tall(split(wide(parts))))
             for at in range(2):
                 one = head + at
                 inner = grad_scaled[:, at * dim : (at + 1) * dim] * esb[one]
                 more = jnp.sum(inner * xh[one].astype(F32), axis=1, keepdims=True)
                 sigma_ref[g] += jnp.where(lane == hh + at, more, 0.0)
-                wide_x[pl.ds(hh + at, tokens, stride=per), :] = mixed[one] + inner
-
-        loop(per // 2, pair_at)
-        x_in[:, g * per : (g + 1) * per, :] = wide_x[...].reshape(tokens, per, dim).astype(BF16)
-        x_copy(g).start()
+                silus[g, pl.ds(hh + at, tokens, stride=per), :] = mixed[one] + inner
+
+        loop(half // 2, lambda i: pair_at(c * half + 2 * i))
+        second_swap(True, g).wait()
+        loop(half // 2, lambda i: pair_at((1 - c) * half + 2 * i))
         here = slice(g * per, (g + 1) * per)
-        sums = lax.dot_general(
-            rho_ref[g] - sigma_ref[g],
-            jnp.where(lower(tokens), 1.0, 0.0).astype(F32),
-            (((0,), (0,)), ((), ())),
-            precision=HIGH,
-            preferred_element_type=F32,
+        sigma_t = jnp.transpose(sigma_ref[g])
+        sums = dot_ones(
+            jnp.transpose(rho_ref[g]) - sigma_t, jnp.where(lower(tokens), 1.0, 0.0).astype(BF16)
         )
         grad_log = sums + jnp.sum(rows[here, :], axis=1, keepdims=True)
         bias_here = column(bias_ref)[here]
         rate_here = -jnp.exp(column(a_ref)[here])
         value = dt_ref[here, :].astype(F32) + bias_here
         step_here = softplus(value)
-        grad_dt = (jnp.transpose(sigma_ref[g]) / step_here + grad_log * rate_here) * sigmoid(value)
+        grad_dt = (sigma_t / step_here + grad_log * rate_here) * sigmoid(value)
         gdt_ref[here, :] = grad_dt.astype(BF16)
         return (
             jnp.sum(grad_log * step_here, axis=1, keepdims=True) * rate_here,
@@ -650,118 +652,180 @@
             jnp.sum(gskip[here, :], axis=1, keepdims=True),
         )
 
-    def swap_copy(source, target, sems):
+    def last_x(g):
+        x_in[:, g * per : (g + 1) * per, :] = silus[g].reshape(tokens, per, dim).astype(BF16)
+        x_copy(g).start()
+
+    def last_b(g):
+        def pair_at(i):
+            head = g * per + 2 * i
+            s_high, s_low = split(
+                wide([behind[head + at] * ec_ref[pl.ds(head + at, 1), :] for at in range(2)])
+            )
+            x_high = wide([xs_high[head], xs_high[head + 1]])
+            x_low = wide([xs_low[head], xs_low[head + 1]])
+            grad_b[g] += dot_nt(wide([x_high, x_high, x_low]), wide([s_high, s_low, s_high]))
+
+        loop(per // 2, pair_at)
+
+    def near_copy(ref, sems, hop):
+        return pltpu.make_async_remote_copy(
+            src_ref=ref.at[0],
+            dst_ref=ref.at[hop],
+            send_sem=sems[0].at[3 + hop],
+            recv_sem=sems[1].at[3 + hop],
+            device_id={"ctx": z * ring_len + lax.rem(q + hop, ring_len)},
+            device_id_type=MESH,
+        )
+
+    def far_copy(source, target, sems, at):
         return pltpu.make_async_remote_copy(
             src_ref=source,
             dst_ref=target,
-            send_sem=sems[0].at[1],
-            recv_sem=sems[1].at[1],
-            device_id={"fsdp": other},
+            send_sem=sems[0].at[1 + at],
+            recv_sem=sems[1].at[1 + at],
+            device_id=far[at],
             device_id_type=MESH,
         )
 
-    def all_copy(ref, sems, hop):
-        return pltpu.make_async_remote_copy(
-            src_ref=ref.at[0],
-            dst_ref=ref.at[hop],
-            send_sem=sems[0].at[1 + hop],
-            recv_sem=sems[1].at[1 + hop],
-            device_id={"ctx": lax.rem(me + hop, count)},
-            device_id_type=MESH,
-        )
-
     gain_sems, small_sems = (gain_send, gain_recv), (small_send, small_recv)
 
-    def gain_swap_copy():
-        return swap_copy(
-            ggain.at[pl.ds(pl.multiple_of(other * per, per), per)], gain_swap, gain_sems
-        )
-
-    copy_in(0).wait()
+    def gain_far(at):
+        owner = mine if at == 1 else other
+        return far_copy(
+            ggain.at[pl.ds(pl.multiple_of(owner * per, per), per)], gain_swap.at[at], gain_sems, at
+        )
+
+    def small_far(at):
+        return far_copy(small_all.at[0], small_swap.at[at], small_sems, at)
+
+    copy_in(0, 0).wait()
     states(0)
     for hop in range(1, ring_len):
         decay_copy(hop).wait()
+    for at in range(ring_len):
+        decays[at] = jnp.broadcast_to(
+            jnp.sum(jnp.where(own_lane, decay_rows[at, :1, :], 0.0), axis=1, keepdims=True),
+            decays.shape[1:],
+        )
     combine(False, 0)
+    copy_in(0, 1).wait()
     states(1)
     combine(False, 1)
     scores(0)
+    inside(0)
+    copy_in(1, 0).wait()
+    copy_in(2, 0).wait()
+    widen(0)
+    prefixes(False, 0)
     scores(1)
-    inside(0)
-    copy_in(1).wait()
-    copy_in(2).wait()
-    prefixes(False, 0)
-    widen(0)
+    inside(1)
     second_chips(False, 0)
-    inside(1)
+    copy_in(1, 1).wait()
+    copy_in(2, 1).wait()
+    widen(1)
+    gain_copy().wait()
     prefixes(False, 1)
-    widen(1)
     second_chips(False, 1)
-    gain_copy().wait()
     returned(False, 0)
-    second_swap(False, 0).wait()
     gated_norm(0)
     pulled(0)
+    combine(True, 0)
     returned(False, 1)
-    combine(True, 0)
-    second_swap(False, 1).wait()
     gated_norm(1)
+    pulled(1)
+    combine(True, 1)
+    for at in range(3):
+        gain_far(at).start()
+    inside_back(0, 0)
     prefixes(True, 0)
-    pulled(1)
+    inside_back(0, 1)
     second_chips(True, 0)
-    combine(True, 1)
-    gain_swap_copy().start()
-    inside_back(0)
+    inside_back(1, 0)
+    prefixes(True, 1)
+    inside_back(1, 1)
+    for at in range(3):
+        gain_far(at).wait()
+    gain_all[0] = (
+        gain_swap[0]
+        + gain_swap[1]
+        + gain_swap[2]
+        + ggain[pl.ds(pl.multiple_of(mine * per, per), per), :]
+    )
+    second_chips(True, 1)
     returned(True, 0)
-    prefixes(True, 1)
-    gain_swap_copy().wait()
-    gain_all[0] = gain_swap[...] + ggain[pl.ds(pl.multiple_of(mine * per, per), per), :]
-    for hop in range(1, count):
-        all_copy(gain_all, gain_sems, hop).start()
-    inside_back(1)
-    gc_ref[...] = halves[...].astype(BF16)
-    second_chips(True, 1)
-    second_swap(True, 0).wait()
-    sums = [last(0)]
+    for hop in range(1, ring_len):
+        near_copy(gain_all, gain_sems, hop).start()
+    sums = [last_sums(0)]
+    last_x(0)
     returned(True, 1)
-    second_swap(True, 1).wait()
-    sums.append(last(1))
-    turn = lax.broadcasted_iota(jnp.int32, (per, dim), 0) == lax.broadcasted_iota(
-        jnp.int32, (per, dim), 1
-    )
+    sums.append(last_sums(1))
     shifted = lax.broadcasted_iota(jnp.int32, (per, dim), 0) + per == lax.broadcasted_iota(
         jnp.int32, (per, dim), 1
     )
     small_all[0] = jnp.zeros(small_out.shape, F32)
     for at in range(3):
         small_all[0, at : at + 1, :] = jnp.sum(
-            jnp.where(turn, sums[0][at], 0.0) + jnp.where(shifted, sums[1][at], 0.0),
+            jnp.where(own_lane[:per], sums[0][at], 0.0) + jnp.where(shifted, sums[1][at], 0.0),
             axis=0,
             keepdims=True,
         )
-    small_mine = swap_copy(small_all.at[0], small_swap, small_sems)
-    small_mine.start()
+    for at in range(3):
+        small_far(at).start()
+    last_x(1)
+    last_b(0)
+    for at in range(3):
+        small_far(at).wait()
+    small_all[0] += small_swap[0] + small_swap[1] + small_swap[2]
+    for hop in range(1, ring_len):
+        near_copy(small_all, small_sems, hop).start()
+    last_b(1)
+    gc_ref[...] = halves[...].astype(BF16)
     for g in range(groups):
         halves[pl.ds(g, tokens, stride=groups), :] = grad_b[g]
     gb_ref[...] = halves[...].astype(BF16)
-    for hop in range(1, count):
-        all_copy(gain_all, gain_sems, hop).wait()
+    for hop in range(1, ring_len):
+        near_copy(gain_all, gain_sems, hop).wait()
     gain_total = gain_all[0]
-    for hop in range(1, count):
+    for hop in range(1, ring_len):
         gain_total = gain_total + gain_all[hop]
     gain_out[...] = gain_total * scale
-    small_mine.wait()
-    small_all[0] += small_swap[...]
-    for hop in range(1, count):
-        all_copy(small_all, small_sems, hop).start()
-    for hop in range(1, count):
-        all_copy(small_all, small_sems, hop).wait()
+    for hop in range(1, ring_len):
+        near_copy(small_all, small_sems, hop).wait()
     small_total = small_all[0]
-    for hop in range(1, count):
+    for hop in range(1, ring_len):
         small_total = small_total + small_all[hop]
     small_out[...] = small_total * scale
     for g in range(groups):
         gate_copy(g).wait()
         x_copy(g).wait()
+
+
+def store_kernel(gx_in, ggate_in, gdt_in, gb_in, gc_in, small, gain, *refs):
+    outs, held, in_sems, out_sems = refs[:9], refs[9], refs[10], refs[11]
+    cuts = in_sems.shape[0] // 2
+    rows = gx_in.shape[0] // cuts
+    jobs = []
+    for at, (source, target) in enumerate(((gx_in, outs[0]), (ggate_in, outs[1]))):
+        for cut in range(cuts):
+            place, one = pl.ds(cut * rows, rows), at * cuts + cut
+            jobs.append(
+                (
+                    pltpu.make_async_copy(source.at[place], held.at[one], in_sems.at[one]),
+                    pltpu.make_async_copy(held.at[one], target.at[place], out_sems.at[one]),
+                )
+            )
+    for job in jobs:
+        job[0].start()
+    for a, b in ((gdt_in, outs[2]), (gb_in, outs[3]), (gc_in, outs[4]), (gain, outs[8])):
+        b[...] = a[...]
+    for at in range(3):
+        outs[5 + at][...] = small[at : at + 1, : outs[5].shape[1]]
+    for job in jobs:
+        job[0].wait()
+        job[1].start()
+    for job in jobs:
+        job[1].wait()
 
 
 def per_device(
@@ -830,7 +894,7 @@
         vmem(ring_len, heads, dim),
         vmem(groups, per, dim),
         vmem(heads, dim),
-        vmem(8, dim),
+        vmem(ring_len, 8, dim),
         vmem(groups, tokens, per),
         vmem(groups, tokens, per),
         vmem(tokens, dim),
@@ -842,20 +906,20 @@
         vmem(heads, dim),
         vmem(heads, dim),
         vmem(heads, dim),
-        vmem(per, dim),
-        vmem(count, per, dim),
-        vmem(8, dim),
-        vmem(count, 8, dim),
-        sems((3,)),
+        vmem(3, per, dim),
+        vmem(ring_len, per, dim),
+        vmem(3, 8, dim),
+        vmem(ring_len, 8, dim),
+        sems((3 * groups,)),
         sems((2 * groups,)),
         sems((ring_len,)),
         sems((ring_len,)),
         sems((2 * groups * 9,)),
         sems((2 * groups * 9,)),
-        sems((1 + count,)),
-        sems((1 + count,)),
-        sems((1 + count,)),
-        sems((1 + count,)),
+        sems((3 + ring_len,)),
+        sems((3 + ring_len,)),
+        sems((3 + ring_len,)),
+        sems((3 + ring_len,)),
     ]
     grad_x, ggate, grad_dt, grad_b, grad_c, small, gain = pl.pallas_call(
         functools.partial(mixer_kernel, scale, groups),
@@ -888,16 +952,31 @@
         skip_weight.reshape(1, heads),
         norm_gain.reshape(per, dim),
     )
+    made = (grad_x, ggate, grad_dt, grad_b, grad_c)
+    line = shape((1, heads), F32)
+    cuts = 4
+    outs = pl.pallas_call(
+        store_kernel,
+        in_specs=[anywhere, anywhere] + [whole] * 5,
+        out_specs=[anywhere, anywhere] + [whole] * 7,
+        out_shape=[shape(a.shape, a.dtype) for a in made] + [line] * 3 + [shape((per, dim), F32)],
+        scratch_shapes=[
+            vmem(2 * cuts, tokens // cuts, heads, dim, kind=BF16),
+            sems((2 * cuts,)),
+            sems((2 * cuts,)),
+        ],
+        name="store",
+    )(*made, small, gain)
     return (
-        grad_x[None],
-        ggate[None],
-        grad_dt[None],
-        grad_b.reshape(b_input.shape),
-        grad_c.reshape(c_input.shape),
-        small[0, :heads],
-        small[1, :heads],
-        small[2, :heads],
-        gain.reshape(norm_gain.shape),
+        outs[0][None],
+        outs[1][None],
+        outs[2][None],
+        outs[3].reshape(b_input.shape),
+        outs[4].reshape(c_input.shape),
+        outs[5].reshape(heads),
+        outs[6].reshape(heads),
+        outs[7].reshape(heads),
+        outs[8].reshape(norm_gain.shape),
     )
 
 

time: 105 us -> 89.7 us (0.85)
  local copies, waits for them, and re-layouts: 8.58 us -> 0 us
  Pallas kernels: 95 us -> 88.2 us
    pallas_call x1, Pallas kernels: 95 us -> 82.9 us  [per_device(): pl.pallas_call(functools.partial(mixer_kernel, scale, groups), in_specs=[...]
    unnamed x16 -> x0, local copies, waits for them, and re-layouts: 7.27 us -> none
    pallas_call x0 -> x1, Pallas kernels: none -> 5.29 us  [per_device(): pl.pallas_call(store_kernel, in_specs=[anywhere, anywhere] + [whole] * 5,...]
    squeeze x1 -> x0, local copies, waits for them, and re-layouts: 1.31 us -> none  [per_device(): small[2, :heads]]
where the time goes in v3:
time: 89.7 us; the launch traced here: 89.5 us
  Pallas kernels  88.2 us (98%)
  between operations  1.3 us (1%)
    pallas_call x1, Pallas kernels, per_device(): pl.pallas_call(functools.partial(mixer_kernel, scale, groups), in_specs=[...  82.9 us
    pallas_call x1, Pallas kernels, per_device(): pl.pallas_call(store_kernel, in_specs=[anywhere, anywhere] + [whole] * 5,...  5.29 us

profile of v3, /device:TPU:1, one launch (start us, length us, event | category | flops | bytes accessed | tf_op | source)
XLA Modules:
  0.0 89.5 jit_solution(14022163636646510712)
XLA Ops:
  1.3 82.9 %mixer.1 = (bf16[256,32,128]{2,1,0:T(8,128)(2,1)}, bf16[256,32,128]{2,1,0:T(8,128)(2,1)}, bf16[32,256]{1,0:T(8,128)(2,1)}, bf16[512,128]{1,0:T(8,128)(2,1)}, bf1...) custom-call(s32[1]{0:T(128)S(6)} %sub.7.limit_ref, bf16[256,32,128]{2,1,0:T(8,128)(2,1)} %bitcast.20, ...), custom_call_target="tpu_custom_call" | custom-call | tf_op jit(solution)/shard_map/mixer/pallas_call | solution.py:924
  84.2 5.3 %store.1 = (bf16[256,32,128]{2,1,0:T(8,128)(2,1)}, bf16[256,32,128]{2,1,0:T(8,128)(2,1)}, bf16[32,256]{1,0:T(8,128)(2,1)}, bf16[512,128]{1,0:T(8,128)(2,1)}, bf1...) custom-call(bf16[256,32,128]{2,1,0:T(8,128)(2,1)} %get-tuple-element.25.g, ...), custom_call_target="tpu_custom_call" | custom-call | tf_op jit(solution)/shard_map/store/pallas_call | solution.py:958

commit v4 on v3

--- a/solution.py
+++ b/solution.py
@@ -72,6 +72,20 @@
     x_hbm,
     gate_hbm,
     out_hbm,
+    dt_hbm,
+    b_hbm,
+    c_hbm,
+    a_hbm,
+    bias_hbm,
+    skip_hbm,
+    gain_hbm,
+    gx_hbm,
+    ggate_hbm,
+    gdt_hbm,
+    gb_hbm,
+    gc_hbm,
+    small_hbm,
+    gain_out_hbm,
     dt_ref,
     b_ref,
     c_ref,
@@ -79,8 +93,6 @@
     bias_ref,
     skip_ref,
     gain_ref,
-    gx_hbm,
-    ggate_hbm,
     gdt_ref,
     gb_ref,
     gc_ref,
@@ -122,6 +134,8 @@
     gains,
     skip_line,
     decay_rows,
+    chip_rows,
+    chains,
     rho_ref,
     sigma_ref,
     square,
@@ -139,6 +153,8 @@
     small_all,
     in_sem,
     out_sem,
+    lead_sem,
+    tail_sem,
     decay_send,
     decay_recv,
     send_sem,
@@ -169,7 +185,39 @@
             source.at[:, place, :], target.at[:, place, :], in_sem.at[at * groups + g]
         )
 
-    for at in range(3):
+    leads = [
+        pltpu.make_async_copy(source, target, lead_sem.at[at])
+        for at, (source, target) in enumerate(
+            (
+                (dt_hbm, dt_ref),
+                (a_hbm, a_ref),
+                (bias_hbm, bias_ref),
+                (skip_hbm, skip_ref),
+                (b_hbm, b_ref),
+                (gain_hbm, gain_ref),
+                (c_hbm, c_ref),
+            )
+        )
+    ]
+    tails = [
+        pltpu.make_async_copy(source, target, tail_sem.at[at])
+        for at, (source, target) in enumerate(
+            (
+                (gdt_ref, gdt_hbm),
+                (gb_ref, gb_hbm),
+                (gc_ref, gc_hbm),
+                (small_out, small_hbm),
+                (gain_out, gain_out_hbm),
+            )
+        )
+    ]
+    for lead in leads[:4]:
+        lead.start()
+    copy_in(0, 0).start()
+    for lead in leads[4:]:
+        lead.start()
+    copy_in(0, 1).start()
+    for at in range(1, 3):
         for g in range(groups):
             copy_in(at, g).start()
     barrier = pltpu.get_barrier_semaphore()
@@ -178,13 +226,18 @@
         {"ctx": (1 - z) * ring_len + q},
         {"ctx": (1 - z) * ring_len + q, "fsdp": other},
     ]
-    for peer in (far[0], far[2]):
+    for peer in far:
         pl.semaphore_signal(barrier, inc=1, device_id=peer, device_id_type=MESH)
-    for hop in range(1, count):
+    for hop in range(1, ring_len):
         pl.semaphore_signal(
-            barrier, inc=1, device_id={"ctx": lax.rem(me + hop, count)}, device_id_type=MESH
-        )
-
+            barrier,
+            inc=1,
+            device_id={"ctx": z * ring_len + lax.rem(q + hop, ring_len)},
+            device_id_type=MESH,
+        )
+
+    for lead in leads:
+        lead.wait()
     diagonal = lax.broadcasted_iota(jnp.int32, (heads, heads), 0) == lax.broadcasted_iota(
         jnp.int32, (heads, heads), 1
     )
@@ -208,17 +261,7 @@
         jnp.int32, (heads, dim), 1
     )
     decay_row = jnp.sum(jnp.where(own_lane, ec * ec, 0.0), axis=0, keepdims=True)
-    decay_rows[q] = jnp.broadcast_to(decay_row, decay_rows.shape[1:])
-
-    def decay_copy(hop):
-        return pltpu.make_async_remote_copy(
-            src_ref=decay_rows.at[q],
-            dst_ref=decay_rows.at[q],
-            send_sem=decay_send.at[hop],
-            recv_sem=decay_recv.at[hop],
-            device_id={"ctx": z * ring_len + lax.rem(q + hop, ring_len)},
-            device_id_type=MESH,
-        )
+    decay_rows[c] = jnp.broadcast_to(decay_row, decay_rows.shape[1:])
 
     def gain_copy():
         return pltpu.make_async_remote_copy(
@@ -261,6 +304,45 @@
     def ring_device(hop):
         return z * ring_len + lax.rem(y + hop, RING) * CORES + c
 
+    def sibling_decay():
+        return pltpu.make_async_remote_copy(
+            src_ref=decay_rows.at[c],
+            dst_ref=decay_rows.at[c],
+            send_sem=decay_send.at[0],
+            recv_sem=decay_recv.at[0],
+            device_id={"ctx": sibling},
+            device_id_type=MESH,
+        )
+
+    def chip_decay(hop):
+        return pltpu.make_async_remote_copy(
+            src_ref=chip_rows.at[y],
+            dst_ref=chip_rows.at[y],
+            send_sem=decay_send.at[hop],
+            recv_sem=decay_recv.at[hop],
+            device_id={"ctx": ring_device(hop)},
+            device_id_type=MESH,
+        )
+
+    def spread(row):
+        return jnp.broadcast_to(
+            jnp.sum(jnp.where(own_lane, row, 0.0), axis=1, keepdims=True), (heads, dim)
+        )
+
+    def core_decays():
+        sibling_decay().wait()
+        chip_rows[y] = decay_rows[0] * decay_rows[1]
+        for hop in range(1, RING):
+            chip_decay(hop).start()
+        for core in range(CORES):
+            decays[core] = spread(decay_rows[core, :1, :])
+
+    def chip_decays():
+        for hop in range(1, RING):
+            chip_decay(hop).wait()
+        for chip in range(RING):
+            chains[chip] = spread(chip_rows[chip, :1, :])
+
     def first_swap(later, g):
         source = local if later else fresh
         return remote(
@@ -322,7 +404,7 @@
 
         def one(k):
             head = g * per + c * half + k
-            decay = decays[y * CORES + second, pl.ds(head, 1), :]
+            decay = decays[second, pl.ds(head, 1), :]
             is_second = c == second
             mul_own = jnp.where(is_second, 1.0, decay)
             mul_sib = jnp.where(is_second, decay, 1.0)
@@ -343,7 +425,7 @@
             head = g * per + c * half + y * own + j
             state = jnp.zeros_like(scat[0])
             for chip in order:
-                decay = decays[chip * CORES, pl.ds(head, 1), :] * decays[chip * CORES + 1, pl.ds(head, 1), :]
+                decay = chains[chip, pl.ds(head, 1), :]
                 pref[g * half + chip * own + j] = state
                 state = scat[g * half + chip * own + j] + decay * state
             total[g * own + j] = state
@@ -363,7 +445,7 @@
                 head = g * per + c * half + y * own + j
                 state = ztotal[g * own + j]
                 for chip in order:
-                    decay = decays[chip * CORES, pl.ds(head, 1), :] * decays[chip * CORES + 1, pl.ds(head, 1), :]
+                    decay = chains[chip, pl.ds(head, 1), :]
                     pref[g * half + chip * own + j] += state
                     state = decay * state
             for hop in range(1, RING):
@@ -384,7 +466,7 @@
 
         def one(k):
             head = g * per + c * half + k
-            decay = decays[y * CORES + first, pl.ds(head, 1), :]
+            decay = decays[first, pl.ds(head, 1), :]
             is_first = c == first
             before = ret[g * half + k]
             base = jnp.where(is_first, source[head], sib[g * half + k])
@@ -420,11 +502,10 @@
 
         loop(half // 2, lambda i: pair_at((1 - c) * half + 2 * i))
         if g == 0:
-            pl.semaphore_wait(barrier, count + 1)
+            pl.semaphore_wait(barrier, ring_len + 2)
+            sibling_decay().start()
         first_swap(False, g).start()
         if g == 0:
-            for hop in range(1, ring_len):
-                decay_copy(hop).start()
             gain_copy().start()
         loop(half // 2, lambda i: pair_at(c * half + 2 * i))
 
@@ -508,14 +589,14 @@
 
     lane = lax.broadcasted_iota(jnp.int32, (tokens, per), 1)
 
-    def put(ref, g, hh, value):
-        ref[g] = jnp.where(lane == hh, value, ref[g])
+    def put(ref, g, hh, values):
+        ref[g] = jnp.where(lane == hh, values[0], jnp.where(lane == hh + 1, values[1], ref[g]))
 
     def pulled(g):
         rho_ref[g] = jnp.zeros((tokens, per), F32)
 
         def pair_at(hh):
-            right = []
+            right, rhos = [], []
             for at in range(2):
                 head = g * per + hh + at
                 row = pl.ds(head, 1)
@@ -533,17 +614,13 @@
                 x_one = xh[head].astype(F32)
                 skip = skip_line[row, :]
                 gskip[row, :] = jnp.sum(grad_mix * x_one, axis=0, keepdims=True)
-                put(
-                    rho_ref,
-                    g,
-                    hh + at,
-                    jnp.sum(grad_mix * (mix - x_one * skip), axis=1, keepdims=True),
-                )
+                rhos.append(jnp.sum(grad_mix * (mix - x_one * skip), axis=1, keepdims=True))
                 mixed[head] = grad_mix * skip
                 high, low = split(grad_mix * erb[head])
                 y_high[head] = high
                 y_low[head] = low
                 right.append(tall([high, low]))
+            put(rho_ref, g, hh, rhos)
             back = dot(ctct[g], wide(right))
             for at in range(2):
                 head = g * per + hh + at
@@ -577,6 +654,7 @@
 
         def pair_at(i):
             hh = part * half + 2 * i
+            sigmas = []
             head = g * per + hh
             yh = wide([y_high[head], y_high[head + 1]])
             yl = wide([y_low[head], y_low[head + 1]])
@@ -594,15 +672,11 @@
             for at in range(2):
                 one = head + at
                 inner = grad_scaled[:, at * dim : (at + 1) * dim] * esb[one]
-                put(
-                    sigma_ref,
-                    g,
-                    hh + at,
-                    jnp.sum(inner * xh[one].astype(F32), axis=1, keepdims=True),
-                )
+                sigmas.append(jnp.sum(inner * xh[one].astype(F32), axis=1, keepdims=True))
                 mixed[one] += inner
                 decay = ec_ref[pl.ds(one, 1), :]
                 fresh[one] += (decay * decay) * carried[one]
+            put(sigma_ref, g, hh, sigmas)
 
         loop(half // 2, pair_at)
         if part == 0:
@@ -617,7 +691,7 @@
     def last_sums(g):
         def pair_at(hh):
             head = g * per + hh
-            parts = []
+            parts, more = [], []
             for at in range(2):
                 one = head + at
                 decay = ec_ref[pl.ds(one, 1), :]
@@ -627,9 +701,9 @@
             for at in range(2):
                 one = head + at
                 inner = grad_scaled[:, at * dim : (at + 1) * dim] * esb[one]
-                more = jnp.sum(inner * xh[one].astype(F32), axis=1, keepdims=True)
-                sigma_ref[g] += jnp.where(lane == hh + at, more, 0.0)
+                more.append(jnp.sum(inner * xh[one].astype(F32), axis=1, keepdims=True))
                 silus[g, pl.ds(hh + at, tokens, stride=per), :] = mixed[one] + inner
+            sigma_ref[g] += jnp.where(lane == hh, more[0], jnp.where(lane == hh + 1, more[1], 0.0))
 
         loop(half // 2, lambda i: pair_at(c * half + 2 * i))
         second_swap(True, g).wait()
@@ -701,13 +775,7 @@
 
     copy_in(0, 0).wait()
     states(0)
-    for hop in range(1, ring_len):
-        decay_copy(hop).wait()
-    for at in range(ring_len):
-        decays[at] = jnp.broadcast_to(
-            jnp.sum(jnp.where(own_lane, decay_rows[at, :1, :], 0.0), axis=1, keepdims=True),
-            decays.shape[1:],
-        )
+    core_decays()
     combine(False, 0)
     copy_in(0, 1).wait()
     states(1)
@@ -717,6 +785,7 @@
     copy_in(1, 0).wait()
     copy_in(2, 0).wait()
     widen(0)
+    chip_decays()
     prefixes(False, 0)
     scores(1)
     inside(1)
@@ -735,15 +804,15 @@
     gated_norm(1)
     pulled(1)
     combine(True, 1)
+    prefixes(True, 0)
     for at in range(3):
         gain_far(at).start()
     inside_back(0, 0)
-    prefixes(True, 0)
+    second_chips(True, 0)
     inside_back(0, 1)
-    second_chips(True, 0)
+    prefixes(True, 1)
     inside_back(1, 0)
-    prefixes(True, 1)
-    inside_back(1, 1)
+    second_chips(True, 1)
     for at in range(3):
         gain_far(at).wait()
     gain_all[0] = (
@@ -752,14 +821,15 @@
         + gain_swap[2]
         + ggain[pl.ds(pl.multiple_of(mine * per, per), per), :]
     )
-    second_chips(True, 1)
-    returned(True, 0)
     for hop in range(1, ring_len):
         near_copy(gain_all, gain_sems, hop).start()
+    returned(True, 0)
+    inside_back(1, 1)
     sums = [last_sums(0)]
     last_x(0)
     returned(True, 1)
     sums.append(last_sums(1))
+    tails[0].start()
     shifted = lax.broadcasted_iota(jnp.int32, (per, dim), 0) + per == lax.broadcasted_iota(
         jnp.int32, (per, dim), 1
     )
@@ -781,51 +851,63 @@
         near_copy(small_all, small_sems, hop).start()
     last_b(1)
     gc_ref[...] = halves[...].astype(BF16)
+    tails[2].start()
     for g in range(groups):
         halves[pl.ds(g, tokens, stride=groups), :] = grad_b[g]
     gb_ref[...] = halves[...].astype(BF16)
+    tails[1].start()
     for hop in range(1, ring_len):
         near_copy(gain_all, gain_sems, hop).wait()
     gain_total = gain_all[0]
     for hop in range(1, ring_len):
         gain_total = gain_total + gain_all[hop]
     gain_out[...] = gain_total * scale
+    tails[4].start()
     for hop in range(1, ring_len):
         near_copy(small_all, small_sems, hop).wait()
     small_total = small_all[0]
     for hop in range(1, ring_len):
         small_total = small_total + small_all[hop]
     small_out[...] = small_total * scale
+    tails[3].start()
     for g in range(groups):
         gate_copy(g).wait()
         x_copy(g).wait()
-
-
-def store_kernel(gx_in, ggate_in, gdt_in, gb_in, gc_in, small, gain, *refs):
-    outs, held, in_sems, out_sems = refs[:9], refs[9], refs[10], refs[11]
-    cuts = in_sems.shape[0] // 2
+    for tail in tails:
+        tail.wait()
+
+
+def store_kernel(gx_in, ggate_in, gdt_in, gb_in, gc_in, small_in, gain_in, *refs):
+    outs = refs[:9]
+    held, gdt, gb, gc, small, gain, lines, in_sems, out_sems = refs[9:]
+    cuts = held.shape[0] // 2
     rows = gx_in.shape[0] // cuts
     jobs = []
     for at, (source, target) in enumerate(((gx_in, outs[0]), (ggate_in, outs[1]))):
         for cut in range(cuts):
-            place, one = pl.ds(cut * rows, rows), at * cuts + cut
-            jobs.append(
-                (
-                    pltpu.make_async_copy(source.at[place], held.at[one], in_sems.at[one]),
-                    pltpu.make_async_copy(held.at[one], target.at[place], out_sems.at[one]),
-                )
-            )
-    for job in jobs:
-        job[0].start()
-    for a, b in ((gdt_in, outs[2]), (gb_in, outs[3]), (gc_in, outs[4]), (gain, outs[8])):
-        b[...] = a[...]
+            place = pl.ds(cut * rows, rows)
+            jobs.append((source.at[place], held.at[at * cuts + cut], target.at[place]))
+    jobs += [(gdt_in, gdt, outs[2]), (gb_in, gb, outs[3]), (gc_in, gc, outs[4])]
+    jobs.append((gain_in, gain, outs[8]))
+    count = len(jobs)
+    into = [pltpu.make_async_copy(job[0], job[1], in_sems.at[at]) for at, job in enumerate(jobs)]
+    away = [pltpu.make_async_copy(job[1], job[2], out_sems.at[at]) for at, job in enumerate(jobs)]
+    lead = pltpu.make_async_copy(small_in, small, in_sems.at[count])
+    lead.start()
+    for copy in into:
+        copy.start()
+    lead.wait()
     for at in range(3):
-        outs[5 + at][...] = small[at : at + 1, : outs[5].shape[1]]
-    for job in jobs:
-        job[0].wait()
-        job[1].start()
-    for job in jobs:
-        job[1].wait()
+        lines[at] = small[at : at + 1, : lines.shape[2]]
+        away.append(
+            pltpu.make_async_copy(lines.at[at], outs[5 + at], out_sems.at[count + at])
+        )
+        away[-1].start()
+    for at in range(count):
+        into[at].wait()
+        away[at].start()
+    for copy in away:
+        copy.wait()
 
 
 def per_device(
@@ -849,7 +931,6 @@
     count = lax.axis_size("ctx")
     ring_len = RING * CORES
     shape = jax.ShapeDtypeStruct
-    whole = pl.BlockSpec(memory_space=pltpu.VMEM)
     anywhere = pl.BlockSpec(memory_space=pl.ANY)
     limit = valid_len - lax.axis_index("ctx") * tokens
     scale = 1.0 / math.sqrt(tokens * count * lax.axis_size("fsdp"))
@@ -859,6 +940,18 @@
         return pltpu.VMEM(dims, kind)
 
     scratch = [
+        vmem(heads, tokens, kind=BF16),
+        vmem(tokens * groups, state, kind=BF16),
+        vmem(tokens * groups, state, kind=BF16),
+        vmem(1, heads),
+        vmem(1, heads),
+        vmem(1, heads),
+        vmem(per, dim),
+        vmem(heads, tokens, kind=BF16),
+        vmem(tokens * groups, state, kind=BF16),
+        vmem(tokens * groups, state, kind=BF16),
+        vmem(8, dim),
+        vmem(per, dim),
         vmem(tokens, heads, dim, kind=BF16),
         vmem(tokens, heads, dim, kind=BF16),
         vmem(tokens, heads, dim, kind=BF16),
@@ -891,10 +984,12 @@
         vmem(groups, tokens, 2 * state, kind=BF16),
         vmem(groups, state, 2 * tokens, kind=BF16),
         vmem(heads, dim),
-        vmem(ring_len, heads, dim),
+        vmem(CORES, heads, dim),
         vmem(groups, per, dim),
         vmem(heads, dim),
-        vmem(ring_len, 8, dim),
+        vmem(CORES, 8, dim),
+        vmem(RING, 8, dim),
+        vmem(RING, heads, dim),
         vmem(groups, tokens, per),
         vmem(groups, tokens, per),
         vmem(tokens, dim),
@@ -912,6 +1007,8 @@
         vmem(ring_len, 8, dim),
         sems((3 * groups,)),
         sems((2 * groups,)),
+        sems((7,)),
+        sems((5,)),
         sems((ring_len,)),
         sems((ring_len,)),
         sems((2 * groups * 9,)),
@@ -923,8 +1020,8 @@
     ]
     grad_x, ggate, grad_dt, grad_b, grad_c, small, gain = pl.pallas_call(
         functools.partial(mixer_kernel, scale, groups),
-        in_specs=[pl.BlockSpec(memory_space=pltpu.SMEM), anywhere, anywhere, anywhere] + [whole] * 7,
-        out_specs=[anywhere, anywhere] + [whole] * 5,
+        in_specs=[pl.BlockSpec(memory_space=pltpu.SMEM), ] + [anywhere] * 10,
+        out_specs=[anywhere] * 7,
         out_shape=[
             shape((tokens, heads, dim), BF16),
             shape((tokens, heads, dim), BF16),
@@ -957,13 +1054,19 @@
     cuts = 4
     outs = pl.pallas_call(
         store_kernel,
-        in_specs=[anywhere, anywhere] + [whole] * 5,
-        out_specs=[anywhere, anywhere] + [whole] * 7,
+        in_specs=[anywhere] * 7,
+        out_specs=[anywhere] * 9,
         out_shape=[shape(a.shape, a.dtype) for a in made] + [line] * 3 + [shape((per, dim), F32)],
         scratch_shapes=[
             vmem(2 * cuts, tokens // cuts, heads, dim, kind=BF16),
-            sems((2 * cuts,)),
-            sems((2 * cuts,)),
+            vmem(heads, tokens, kind=BF16),
+            vmem(tokens * groups, state, kind=BF16),
+            vmem(tokens * groups, state, kind=BF16),
+            vmem(8, dim),
+            vmem(per, dim),
+            vmem(3, 1, heads),
+            sems((2 * cuts + 5,)),
+            sems((2 * cuts + 7,)),
         ],
         name="store",
     )(*made, small, gain)

time: 89.7 us -> 85.6 us (0.954)
  Pallas kernels: 88.2 us -> 83.9 us
    pallas_call x1, Pallas kernels: 82.9 us -> 80 us  [per_device(): pl.pallas_call(functools.partial(mixer_kernel, scale, groups), in_specs=[...]
    pallas_call x1, Pallas kernels: 5.29 us -> 3.84 us  [per_device(): pl.pallas_call(store_kernel, in_specs=[anywhere] * 7, out_specs=[anywhere...]
where the time goes in v4:
time: 85.6 us; the launch traced here: 85.3 us
  Pallas kernels  83.9 us (98%)
  between operations  1.47 us (2%)
    pallas_call x1, Pallas kernels, per_device(): pl.pallas_call(functools.partial(mixer_kernel, scale, groups), in_specs=[...  80 us
    pallas_call x1, Pallas kernels, per_device(): pl.pallas_call(store_kernel, in_specs=[anywhere] * 7, out_specs=[anywhere...  3.84 us

profile of v4, /device:TPU:1, one launch (start us, length us, event | category | flops | bytes accessed | tf_op | source)
XLA Modules:
  0.0 85.3 jit_solution(17139044542905139419)
XLA Ops:
  1.3 80.0 %mixer.1 = (bf16[256,32,128]{2,1,0:T(8,128)(2,1)}, bf16[256,32,128]{2,1,0:T(8,128)(2,1)}, bf16[32,256]{1,0:T(8,128)(2,1)}, bf16[512,128]{1,0:T(8,128)(2,1)}, bf1...) custom-call(s32[1]{0:T(128)S(6)} %sub.7.limit_ref, bf16[256,32,128]{2,1,0:T(8,128)(2,1)} %bitcast.20, ...), custom_call_target="tpu_custom_call" | custom-call | tf_op jit(solution)/shard_map/mixer/pallas_call | solution.py:1021
  81.3 3.8 %store.1 = (bf16[256,32,128]{2,1,0:T(8,128)(2,1)}, bf16[256,32,128]{2,1,0:T(8,128)(2,1)}, bf16[32,256]{1,0:T(8,128)(2,1)}, bf16[512,128]{1,0:T(8,128)(2,1)}, bf1...) custom-call(bf16[256,32,128]{2,1,0:T(8,128)(2,1)} %get-tuple-element.25.g, ...), custom_call_target="tpu_custom_call" | custom-call | tf_op jit(solution)/shard_map/store/pallas_call | solution.py:1055

commit v5 on v4

--- a/solution.py
+++ b/solution.py
@@ -805,10 +805,10 @@
     pulled(1)
     combine(True, 1)
     prefixes(True, 0)
+    inside_back(0, 0)
+    second_chips(True, 0)
     for at in range(3):
         gain_far(at).start()
-    inside_back(0, 0)
-    second_chips(True, 0)
     inside_back(0, 1)
     prefixes(True, 1)
     inside_back(1, 0)

time: 85.6 us -> 85.6 us (level)
  no operation moved by 1% of the time
where the time goes in v5:
time: 85.6 us; the launch traced here: 85.3 us
  Pallas kernels  83.9 us (98%)
  between operations  1.47 us (2%)
    pallas_call x1, Pallas kernels, per_device(): pl.pallas_call(functools.partial(mixer_kernel, scale, groups), in_specs=[...  80 us
    pallas_call x1, Pallas kernels, per_device(): pl.pallas_call(store_kernel, in_specs=[anywhere] * 7, out_specs=[anywhere...  3.84 us

profile of v5, /device:TPU:1, one launch (start us, length us, event | category | flops | bytes accessed | tf_op | source)
XLA Modules:
  0.0 85.3 jit_solution(5024278346712558039)
XLA Ops:
  1.3 80.0 %mixer.1 = (bf16[256,32,128]{2,1,0:T(8,128)(2,1)}, bf16[256,32,128]{2,1,0:T(8,128)(2,1)}, bf16[32,256]{1,0:T(8,128)(2,1)}, bf16[512,128]{1,0:T(8,128)(2,1)}, bf1...) custom-call(s32[1]{0:T(128)S(6)} %sub.7.limit_ref, bf16[256,32,128]{2,1,0:T(8,128)(2,1)} %bitcast.20, ...), custom_call_target="tpu_custom_call" | custom-call | tf_op jit(solution)/shard_map/mixer/pallas_call | solution.py:1021
  81.3 3.8 %store.1 = (bf16[256,32,128]{2,1,0:T(8,128)(2,1)}, bf16[256,32,128]{2,1,0:T(8,128)(2,1)}, bf16[32,256]{1,0:T(8,128)(2,1)}, bf16[512,128]{1,0:T(8,128)(2,1)}, bf1...) custom-call(bf16[256,32,128]{2,1,0:T(8,128)(2,1)} %get-tuple-element.25.g, ...), custom_call_target="tpu_custom_call" | custom-call | tf_op jit(solution)/shard_map/store/pallas_call | solution.py:1055
